TPU v7x, 32 devices: a whole 2x2x4 slice. The times are simulated.
32 devices in a mesh: section: 2 (over x), dp: 4 (over z), mp: 4 (over y, core).
Axes of the slice: x: 2, y: 2, z: 4, core: 2. Of those that a mesh axis runs over, the one named last changes fastest.
Arguments:
- inputs: bfloat16 [2, 4096, 768], P(None, ('dp', 'mp')), may hold values from -6 to 6
- cotangent: bfloat16 [2, 4096, 768], P(None, ('dp', 'mp')), may hold values from -6 to 6
- w_query: bfloat16 [2, 768, 768], P('section', 'dp', 'mp'), may hold values from -0.21875 to 0.21875
- w_key: bfloat16 [2, 768, 768], P('section', 'dp', 'mp'), may hold values from -0.21875 to 0.21875
- w_value: bfloat16 [2, 768, 768], P('section', 'dp', 'mp'), may hold values from -0.21875 to 0.21875
- w_attn_out: bfloat16 [2, 768, 768], P('section', 'mp', 'dp'), may hold values from -2.5 to 2.5
- rel_table: bfloat16 [2, 12, 32], P('section', 'mp', 'dp'), may hold values from -4 to 4
- gain_attn: bfloat16 [2, 768], P('section'), may hold values from 0.5 to 1.5
- gain_ffn: bfloat16 [2, 768], P('section'), may hold values from 0.5 to 1.5
- w_router: bfloat16 [2, 768, 8], P('section'), may hold values from -0.15625 to 0.15625
- w_expert_in: bfloat16 [2, 8, 768, 3072], P('section', None, 'dp', 'mp'), may hold values from -0.21875 to 0.21875
- w_expert_out: bfloat16 [2, 8, 3072, 768], P('section', None, 'mp', 'dp'), may hold values from -0.875 to 0.875
- doc_ids: int32 [2, 4096], P(None, 'dp'), may hold values from 0 to 2, as said below
- expert_ids: int32 [2, 4096, 1], P(None, 'dp'), may hold values from 0 to 7; in each aligned block of 1024 rows (0 to 1023, 1024 to 2047, ..., all dimensions but the last counted through in order) at most 256 rows name the same one
- buckets: int32 [2047], replicated, may hold values from 0 to 31
Outputs:
- section_outputs: bfloat16 [2, 2, 4096, 768], P('section', None, ('dp', 'mp'))
- grad_inputs: float32 [2, 2, 4096, 768], P('section', None, ('dp', 'mp'))
- grad_query: float32 [2, 768, 768], P('section', 'dp', 'mp')
- grad_key: float32 [2, 768, 768], P('section', 'dp', 'mp')
- grad_value: float32 [2, 768, 768], P('section', 'dp', 'mp')
- grad_attn_out: float32 [2, 768, 768], P('section', 'mp', 'dp')
- grad_rel_table: float32 [2, 12, 32], P('section', 'mp', 'dp')
- grad_gain_attn: float32 [2, 768], P('section', ('dp', 'mp'))
- grad_gain_ffn: float32 [2, 768], P('section', ('dp', 'mp'))
- grad_router: float32 [2, 768, 8], P('section', ('dp', 'mp'))
- grad_expert_in: float32 [2, 8, 768, 3072], P('section', None, 'dp', 'mp')
- grad_expert_out: float32 [2, 8, 3072, 768], P('section', None, 'mp', 'dp')
Inputs may be any that keep to these rules, and one draw needn't show every extreme that they name: `doc_ids`: within one micro-batch and group of 1024 tokens the document numbers never fall and take 0, 1 and 2, each at least once; document 1 holds more than 768 tokens. `expert_ids`: within one micro-batch and group of 1024 tokens no expert is named by more than 256 tokens; in some groups one is named by exactly 256.
All inputs are finite; a program needn't handle non-finite values.
Results may differ from a plain program's by a relative error of at most 0.025.
Values may be sent and summed in bfloat16 or wider, within the bound.
A program may use at most 256 MiB of HBM per device.

v0:
```python
import jax
import jax.numpy as jnp
from jax import lax
from jax.sharding import PartitionSpec as P


def shifted(value, axis, steps):
    count = lax.axis_size(axis)
    initial, last = (max(0, -steps), min(count, count - steps))
    return lax.ppermute(value, axis, [(source, source + steps) for source in range(initial, last)])


def normed(values, gain):
    return values * lax.rsqrt(jnp.mean(values * values, axis=-1, keepdims=True) + 1e-06) * gain


def bucket_onehot(buckets, count):
    return (buckets[:, None] == jnp.arange(count, dtype=jnp.int32)[None, :]).astype(jnp.float32)


def slots_of(chosen, capacity, experts):
    onehot = (chosen[:, None] == jnp.arange(experts, dtype=jnp.int32)[None, :]).astype(jnp.int32)
    rank = jnp.sum((jnp.cumsum(onehot, axis=0) - 1) * onehot, axis=1)
    return chosen * capacity + rank


def skewed_bias(bias_off, opening, block_len, group_len):
    head_count = bias_off.shape[0]
    span = group_len + block_len - 1
    window = lax.dynamic_slice_in_dim(bias_off, group_len - block_len - opening, span, 1)
    tiled = jnp.broadcast_to(window[:, None, :], (head_count, block_len, span)).reshape(
        head_count, block_len * span
    )
    tiled = jnp.pad(tiled, ((0, 0), (0, block_len))).reshape(head_count, block_len, span + 1)[
        :, :, :group_len
    ]
    return tiled[:, ::-1, :]


def diagonal_sums(grad_scores, block_len, group_len):
    head_count = grad_scores.shape[0]
    span = group_len + block_len - 1
    flipped = grad_scores[:, ::-1, :]
    padded = jnp.pad(flipped, ((0, 0), (0, 0), (0, block_len))).reshape(
        head_count, block_len * (span + 1)
    )
    padded = padded[:, : block_len * span].reshape(head_count, block_len, span)
    return jnp.sum(padded, axis=1)


def block_scores(query_rows, key_rows, bias_off, doc_rows, documents, opening):
    group_len = key_rows.shape[0]
    block_len = query_rows.shape[0]
    scale = query_rows.shape[2] ** (-0.5)
    scores = (
        jnp.einsum("qhd,khd->hqk", query_rows, key_rows, preferred_element_type=jnp.float32) * scale
    )
    scores = scores + skewed_bias(bias_off, opening, block_len, group_len)
    scores = jnp.where((doc_rows[:, None] == documents[None, :])[None], scores, -1e30)
    return scores


def attend(queries, key_rows, value_rows, bias_off, documents):
    group_len = queries.shape[0]
    block_len = min(512, group_len)

    def one_block(opening):
        query_rows = lax.dynamic_slice_in_dim(queries, opening, block_len, 0)
        doc_rows = lax.dynamic_slice_in_dim(documents, opening, block_len, 0)
        scores = block_scores(query_rows, key_rows, bias_off, doc_rows, documents, opening)
        top_score = jnp.max(scores, axis=-1, keepdims=True)
        expo = jnp.exp(scores - top_score)
        total = jnp.sum(expo, axis=-1, keepdims=True)
        weights = (expo / total).astype(jnp.bfloat16)
        mixed = jnp.einsum("hqk,khd->qhd", weights, value_rows, preferred_element_type=jnp.float32)
        return (mixed.astype(jnp.bfloat16), (top_score + jnp.log(total))[..., 0])

    openings = jnp.arange(group_len // block_len, dtype=jnp.int32) * block_len
    mixed, lse_all = lax.map(one_block, openings)
    return (mixed.reshape(group_len, -1), lse_all)


def attend_back(queries, key_rows, value_rows, grad_mixed, lse_all, bias_off, documents):
    group_len, head_count, head_width = queries.shape
    block_len = min(512, group_len)
    scale = head_width ** (-0.5)
    span = group_len + block_len - 1

    def one_block(carry, item):
        grad_keys, grad_values, grad_bias = carry
        opening, lse_rows = item
        query_rows = lax.dynamic_slice_in_dim(queries, opening, block_len, 0)
        doc_rows = lax.dynamic_slice_in_dim(documents, opening, block_len, 0)
        grad_rows = lax.dynamic_slice_in_dim(grad_mixed, opening, block_len, 0)
        scores = block_scores(query_rows, key_rows, bias_off, doc_rows, documents, opening)
        probs = jnp.exp(scores - lse_rows[..., None])
        grad_probs = jnp.einsum(
            "qhd,khd->hqk", grad_rows, value_rows, preferred_element_type=jnp.float32
        )
        inner_sum = jnp.sum(probs * grad_probs, axis=-1, keepdims=True)
        grad_exact = probs * (grad_probs - inner_sum)
        grad_scores = grad_exact.astype(jnp.bfloat16)
        grad_query = (
            jnp.einsum("hqk,khd->qhd", grad_scores, key_rows, preferred_element_type=jnp.float32)
            * scale
        )
        grad_keys = (
            grad_keys
            + jnp.einsum(
                "hqk,qhd->khd", grad_scores, query_rows, preferred_element_type=jnp.float32
            )
            * scale
        )
        grad_values = grad_values + jnp.einsum(
            "hqk,qhd->khd",
            probs.astype(jnp.bfloat16),
            grad_rows,
            preferred_element_type=jnp.float32,
        )
        start = group_len - block_len - opening
        current = lax.dynamic_slice_in_dim(grad_bias, start, span, 1)
        grad_bias = lax.dynamic_update_slice_in_dim(
            grad_bias, current + diagonal_sums(grad_exact, block_len, group_len), start, 1
        )
        return ((grad_keys, grad_values, grad_bias), grad_query)

    zeros_rows = jnp.zeros(queries.shape, jnp.float32)
    start_bias = jnp.zeros(bias_off.shape, jnp.float32)
    openings = jnp.arange(group_len // block_len, dtype=jnp.int32) * block_len
    (grad_keys, grad_values, grad_bias), grad_query = lax.scan(
        one_block, (zeros_rows, zeros_rows, start_bias), (openings, lse_all)
    )
    return (
        grad_query.reshape(group_len, head_count, head_width),
        grad_keys,
        grad_values,
        grad_bias,
    )


def layer_forward(layer_in, documents, chosen, fetched, small, buckets):
    w_query, w_key, w_value, w_attn_out, rel_table, w_expert_in, w_expert_out = fetched
    gain_attn, gain_ffn, w_router = small
    row_count, width = layer_in.shape
    group_len = documents.shape[0]
    head_count = rel_table.shape[0]
    experts = w_expert_in.shape[0]
    capacity = group_len // 4
    mp_index = lax.axis_index("mp")
    normed_attn = normed(layer_in, gain_attn).astype(jnp.bfloat16)
    gathered = lax.all_gather(normed_attn, "mp", axis=0, tiled=True)
    queries = jnp.dot(gathered, w_query, preferred_element_type=jnp.float32).astype(jnp.bfloat16)
    key_rows = jnp.dot(gathered, w_key, preferred_element_type=jnp.float32).astype(jnp.bfloat16)
    value_rows = jnp.dot(gathered, w_value, preferred_element_type=jnp.float32).astype(jnp.bfloat16)
    queries = queries.reshape(group_len, head_count, -1)
    key_rows = key_rows.reshape(group_len, head_count, -1)
    value_rows = value_rows.reshape(group_len, head_count, -1)
    bias_off = jnp.dot(
        rel_table.astype(jnp.float32),
        bucket_onehot(buckets, rel_table.shape[1]).T,
        precision=lax.Precision.HIGHEST,
    )
    mixed, lse_all = attend(queries, key_rows, value_rows, bias_off, documents)
    attn = lax.psum_scatter(
        jnp.dot(mixed, w_attn_out, preferred_element_type=jnp.float32),
        "mp",
        scatter_dimension=0,
        tiled=True,
    )
    hidden = layer_in + attn
    routed_loc = normed(hidden, gain_ffn).astype(jnp.bfloat16)
    routed = lax.all_gather(routed_loc, "mp", axis=0, tiled=True)
    router_prob = jax.nn.softmax(
        jnp.dot(routed_loc, w_router, preferred_element_type=jnp.float32), axis=-1
    )
    chosen_loc = lax.dynamic_slice_in_dim(chosen, mp_index * row_count, row_count, 0)
    picked = (chosen_loc[:, None] == jnp.arange(experts, dtype=jnp.int32)[None, :]).astype(
        jnp.float32
    )
    gate_prob = jnp.sum(router_prob * picked, axis=1, keepdims=True)
    slots = slots_of(chosen, capacity, experts)
    buffer = jnp.zeros((experts * capacity, width), jnp.bfloat16).at[slots].set(routed)
    inner = jnp.einsum(
        "ecd,edf->ecf",
        buffer.reshape(experts, capacity, width),
        w_expert_in,
        preferred_element_type=jnp.float32,
    )
    active = jax.nn.gelu(inner).astype(jnp.bfloat16)
    partial_out = jnp.einsum(
        "ecf,efd->ecd", active, w_expert_out, preferred_element_type=jnp.float32
    )
    expert_out = lax.psum_scatter(
        partial_out.reshape(experts * capacity, width)[slots], "mp", scatter_dimension=0, tiled=True
    )
    result = hidden + gate_prob * expert_out
    kept = (
        layer_in,
        gathered,
        queries,
        key_rows,
        value_rows,
        lse_all,
        mixed,
        hidden,
        routed,
        router_prob,
        picked,
        gate_prob,
        expert_out,
        inner,
        active,
        slots,
        documents,
    )
    return (result, kept)


def ffn_backward(grad_out, kept, fetched, small):
    w_query, w_key, w_value, w_attn_out, rel_table, w_expert_in, w_expert_out = fetched
    gain_attn, gain_ffn, w_router = small
    (
        layer_in,
        gathered,
        queries,
        key_rows,
        value_rows,
        lse_all,
        mixed,
        hidden,
        routed,
        router_prob,
        picked,
        gate_prob,
        expert_out,
        inner,
        active,
        slots,
        documents,
    ) = kept
    row_count, width = layer_in.shape
    group_len = documents.shape[0]
    experts = w_expert_in.shape[0]
    capacity = group_len // 4
    mp_index = lax.axis_index("mp")
    grad_expert_loc = (gate_prob * grad_out).astype(jnp.bfloat16)
    grad_gate = jnp.sum(grad_out * expert_out, axis=1, keepdims=True)
    grad_expert = lax.all_gather(grad_expert_loc, "mp", axis=0, tiled=True)
    grad_buffer = jnp.zeros((experts * capacity, width), jnp.bfloat16).at[slots].set(grad_expert)
    grad_buffer = grad_buffer.reshape(experts, capacity, width)
    grad_active = jnp.einsum(
        "ecd,efd->ecf", grad_buffer, w_expert_out, preferred_element_type=jnp.float32
    )
    grad_w_out = jnp.einsum("ecf,ecd->efd", active, grad_buffer, preferred_element_type=jnp.float32)
    grad_inner = jax.vjp(jax.nn.gelu, inner)[1](grad_active)[0].astype(jnp.bfloat16)
    buffer = jnp.zeros((experts * capacity, width), jnp.bfloat16).at[slots].set(routed)
    grad_w_in = jnp.einsum(
        "ecd,ecf->edf",
        buffer.reshape(experts, capacity, width),
        grad_inner,
        preferred_element_type=jnp.float32,
    )
    grad_routed_part = jnp.einsum(
        "ecf,edf->ecd", grad_inner, w_expert_in, preferred_element_type=jnp.float32
    )
    grad_routed = lax.psum_scatter(
        grad_routed_part.reshape(experts * capacity, width)[slots],
        "mp",
        scatter_dimension=0,
        tiled=True,
    )
    grad_prob = picked * grad_gate
    grad_logit = router_prob * (grad_prob - jnp.sum(router_prob * grad_prob, axis=1, keepdims=True))
    router_full = w_router.astype(jnp.float32)
    grad_routed = grad_routed + jnp.dot(grad_logit, router_full.T, precision=lax.Precision.HIGHEST)
    routed_loc = lax.dynamic_slice_in_dim(routed, mp_index * row_count, row_count, 0).astype(
        jnp.float32
    )
    grad_router = jnp.dot(routed_loc.T, grad_logit, precision=lax.Precision.HIGHEST)
    norm_back = jax.vjp(normed, hidden, gain_ffn)[1]
    grad_hidden_norm, grad_gain_ffn = norm_back(grad_routed)
    grad_hidden = grad_out + grad_hidden_norm
    return (grad_hidden, (grad_w_in, grad_w_out), (grad_gain_ffn, grad_router))


def attn_backward(grad_hidden, kept, fetched, small, buckets):
    w_query, w_key, w_value, w_attn_out, rel_table, w_expert_in, w_expert_out = fetched
    gain_attn, gain_ffn, w_router = small
    (
        layer_in,
        gathered,
        queries,
        key_rows,
        value_rows,
        lse_all,
        mixed,
        hidden,
        routed,
        router_prob,
        picked,
        gate_prob,
        expert_out,
        inner,
        active,
        slots,
        documents,
    ) = kept
    group_len = documents.shape[0]
    grad_attn = lax.all_gather(grad_hidden.astype(jnp.bfloat16), "mp", axis=0, tiled=True)
    grad_w_attn_out = jnp.einsum("tc,td->cd", mixed, grad_attn, preferred_element_type=jnp.float32)
    grad_mixed = jnp.einsum("td,cd->tc", grad_attn, w_attn_out, preferred_element_type=jnp.float32)
    grad_mixed = grad_mixed.astype(jnp.bfloat16).reshape(queries.shape)
    bias_onehot = bucket_onehot(buckets, rel_table.shape[1])
    bias_off = jnp.dot(
        rel_table.astype(jnp.float32), bias_onehot.T, precision=lax.Precision.HIGHEST
    )
    grad_query, grad_keys, grad_values, grad_bias = attend_back(
        queries, key_rows, value_rows, grad_mixed, lse_all, bias_off, documents
    )
    grad_table = jnp.dot(grad_bias, bias_onehot, precision=lax.Precision.HIGHEST)
    grad_query = grad_query.reshape(group_len, -1).astype(jnp.bfloat16)
    grad_keys = grad_keys.reshape(group_len, -1).astype(jnp.bfloat16)
    grad_values = grad_values.reshape(group_len, -1).astype(jnp.bfloat16)
    grad_w_query = jnp.einsum("td,tc->dc", gathered, grad_query, preferred_element_type=jnp.float32)
    grad_w_key = jnp.einsum("td,tc->dc", gathered, grad_keys, preferred_element_type=jnp.float32)
    grad_w_value = jnp.einsum(
        "td,tc->dc", gathered, grad_values, preferred_element_type=jnp.float32
    )
    grad_normed_part = (
        jnp.einsum("tc,dc->td", grad_query, w_query, preferred_element_type=jnp.float32)
        + jnp.einsum("tc,dc->td", grad_keys, w_key, preferred_element_type=jnp.float32)
        + jnp.einsum("tc,dc->td", grad_values, w_value, preferred_element_type=jnp.float32)
    )
    grad_normed = lax.psum_scatter(grad_normed_part, "mp", scatter_dimension=0, tiled=True)
    norm_back_attn = jax.vjp(normed, layer_in, gain_attn)[1]
    grad_in_norm, grad_gain_attn = norm_back_attn(grad_normed)
    grad_in = grad_hidden + grad_in_norm
    return (
        grad_in,
        (grad_w_query, grad_w_key, grad_w_value, grad_w_attn_out, grad_table),
        grad_gain_attn,
    )


def per_device(
    inputs,
    cotangent,
    w_query,
    w_key,
    w_value,
    w_attn_out,
    rel_table,
    gain_attn,
    gain_ffn,
    w_router,
    w_expert_in,
    w_expert_out,
    doc_ids,
    expert_ids,
    buckets,
):
    micro = inputs.shape[0]
    is_first = lax.axis_index("section") == 0
    sharded = (
        w_query[0],
        w_key[0],
        w_value[0],
        w_attn_out[0],
        rel_table[0],
        w_expert_in[0],
        w_expert_out[0],
    )
    fetched = (
        lax.all_gather(sharded[0], "dp", axis=0, tiled=True),
        lax.all_gather(sharded[1], "dp", axis=0, tiled=True),
        lax.all_gather(sharded[2], "dp", axis=0, tiled=True),
        lax.all_gather(sharded[3], "dp", axis=1, tiled=True),
        lax.all_gather(sharded[4], "dp", axis=1, tiled=True),
        lax.all_gather(sharded[5], "dp", axis=1, tiled=True),
        lax.all_gather(sharded[6], "dp", axis=2, tiled=True),
    )
    small = (gain_attn[0].astype(jnp.float32), gain_ffn[0].astype(jnp.float32), w_router[0])
    received = jnp.zeros(inputs.shape[1:], jnp.bfloat16)
    results, stored = ([], [])
    for tick in range(micro + 1):
        early = min(tick, micro - 1)
        later = max(tick - 1, 0)
        layer_in = jnp.where(
            is_first, inputs[early].astype(jnp.float32), received.astype(jnp.float32)
        )
        documents = jnp.where(is_first, doc_ids[early], doc_ids[later])
        chosen = jnp.where(is_first, expert_ids[early, :, 0], expert_ids[later, :, 0])
        result, kept = layer_forward(layer_in, documents, chosen, fetched, small, buckets)
        results.append(result)
        stored.append(kept)
        if tick < micro:
            received = shifted(result.astype(jnp.bfloat16), "section", 1)
    back_weights = (
        lax.all_gather(sharded[0], "dp", axis=0, tiled=True),
        lax.all_gather(sharded[1], "dp", axis=0, tiled=True),
        lax.all_gather(sharded[2], "dp", axis=0, tiled=True),
        lax.all_gather(sharded[3], "dp", axis=1, tiled=True),
        lax.all_gather(sharded[4], "dp", axis=1, tiled=True),
        lax.all_gather(sharded[5], "dp", axis=1, tiled=True),
        lax.all_gather(sharded[6], "dp", axis=2, tiled=True),
    )
    attn_total = tuple((jnp.zeros(weight.shape, jnp.float32) for weight in back_weights[:5]))
    ffn_total = tuple((jnp.zeros(weight.shape, jnp.float32) for weight in back_weights[5:]))
    small_total = (
        jnp.zeros(small[0].shape, jnp.float32),
        jnp.zeros(small[1].shape, jnp.float32),
        jnp.zeros(small[2].shape, jnp.float32),
    )
    returned = jnp.zeros(inputs.shape[1:], jnp.bfloat16)
    grad_list = []
    for tick in range(micro + 1):
        before = stored[max(tick - 1, 0)]
        after = stored[min(tick + 1, micro)]
        kept = jax.tree.map(lambda one, two: jnp.where(is_first, one, two), before, after)
        grad_out = jnp.where(
            is_first,
            returned.astype(jnp.float32),
            cotangent[min(tick, micro - 1)].astype(jnp.float32),
        )
        valid = jnp.where(is_first, 1.0 if tick >= 1 else 0.0, 1.0 if tick < micro else 0.0).astype(
            jnp.float32
        )
        grad_hidden, ffn_grads, ffn_small = ffn_backward(grad_out, kept, back_weights, small)
        ffn_total = jax.tree.map(lambda total, grad: total + valid * grad, ffn_total, ffn_grads)
        grad_in, attn_grads, gain_grad = attn_backward(
            grad_hidden, kept, back_weights, small, buckets
        )
        attn_total = jax.tree.map(lambda total, grad: total + valid * grad, attn_total, attn_grads)
        small_total = (
            small_total[0] + valid * gain_grad,
            small_total[1] + valid * ffn_small[0],
            small_total[2] + valid * ffn_small[1],
        )
        grad_list.append(grad_in)
        if tick < micro:
            returned = shifted(grad_in.astype(jnp.bfloat16), "section", -1)
    big_sum = (
        lax.psum_scatter(attn_total[0], "dp", scatter_dimension=0, tiled=True),
        lax.psum_scatter(attn_total[1], "dp", scatter_dimension=0, tiled=True),
        lax.psum_scatter(attn_total[2], "dp", scatter_dimension=0, tiled=True),
        lax.psum_scatter(attn_total[3], "dp", scatter_dimension=1, tiled=True),
        lax.psum_scatter(attn_total[4], "dp", scatter_dimension=1, tiled=True),
        lax.psum_scatter(ffn_total[0], "dp", scatter_dimension=1, tiled=True),
        lax.psum_scatter(ffn_total[1], "dp", scatter_dimension=2, tiled=True),
    )
    small_sum = (
        lax.psum_scatter(small_total[0], ("dp", "mp"), scatter_dimension=0, tiled=True),
        lax.psum_scatter(small_total[1], ("dp", "mp"), scatter_dimension=0, tiled=True),
        lax.psum_scatter(small_total[2], ("dp", "mp"), scatter_dimension=0, tiled=True),
    )
    outputs = jnp.stack(
        [jnp.where(is_first, results[index], results[index + 1]) for index in range(micro)]
    )
    grad_inputs = jnp.stack(
        [jnp.where(is_first, grad_list[index + 1], grad_list[index]) for index in range(micro)]
    )
    return (
        outputs.astype(jnp.bfloat16)[None],
        grad_inputs[None],
        big_sum[0][None],
        big_sum[1][None],
        big_sum[2][None],
        big_sum[3][None],
        big_sum[4][None],
        small_sum[0][None],
        small_sum[1][None],
        small_sum[2][None],
        big_sum[5][None],
        big_sum[6][None],
    )


def solution(mesh):
    placed = (
        P(None, ("dp", "mp"), None),
        P(None, ("dp", "mp"), None),
        P("section", "dp", "mp"),
        P("section", "dp", "mp"),
        P("section", "dp", "mp"),
        P("section", "mp", "dp"),
        P("section", "mp", "dp"),
        P("section", None),
        P("section", None),
        P("section", None, None),
        P("section", None, "dp", "mp"),
        P("section", None, "mp", "dp"),
        P(None, "dp"),
        P(None, "dp", None),
        P(),
    )
    return jax.shard_map(
        per_device,
        mesh=mesh,
        in_specs=placed,
        out_specs=(
            P("section", None, ("dp", "mp"), None),
            P("section", None, ("dp", "mp"), None),
            P("section", "dp", "mp"),
            P("section", "dp", "mp"),
            P("section", "dp", "mp"),
            P("section", "mp", "dp"),
            P("section", "mp", "dp"),
            P("section", ("dp", "mp")),
            P("section", ("dp", "mp")),
            P("section", ("dp", "mp"), None),
            P("section", None, "dp", "mp"),
            P("section", None, "mp", "dp"),
        ),
        check_vma=False,
    )
```

profile of v0, /device:TPU:0, one launch (start us, length us, event | category | flops | bytes accessed | tf_op | source)
XLA Modules:
  0.0 4444.1 jit_solution(13519588559308457126)
XLA Ops:
  102.8 239.7 %while.99 = (s32[]{:T(128)}, bf16[2,512,3,64]{1,3,2,0:T(8,128)(2,1)}, f32[2,3,512]{2,1,0:T(4,128)S(1)}, s32[2]{0:T(128)S(1)}, s32[1024]{0:T(1024)S(1)}, /*index=...) while((s32[]{:T(128)}, ...), condition=%wide.region_4.5_spmd, body=%wide.region_1.4_spmd.sunk | while | flops 417430016 | bytes 143874384 | solution.py:79
  158.2 48.5 %rev.69 = f32[3,512,1024]{2,1,0:T(8,128)} reverse(f32[3,512,1024]{2,1,0:T(8,128)} %slice.251), dimensions={1} | reverse | bytes 12582912 | tf_op jit(solution)/shard_map/while/body/eval_jaxpr/rev | solution.py:37
  272.8 48.5 %rev.69 = f32[3,512,1024]{2,1,0:T(8,128)} reverse(f32[3,512,1024]{2,1,0:T(8,128)} %slice.251), dimensions={1} | reverse | bytes 12582912 | tf_op jit(solution)/shard_map/while/body/eval_jaxpr/rev | solution.py:37
  347.7 38.3 reduce-scatter.25.cloned.1.call-done
  416.1 161.0 %all-gather.48.cloned.1.call-done = bf16[1,8,768,768]{2,1,0,3:T(8,128)(2,1)} async-done(((bf16[1,8,768,192]{2,1,0,3:T(8,128)(2,1)}), bf16[1,8,768,768]{2,1,0,3:T(8,128)(2,1)}) %all-gather.48.cloned.1.call-update) | async-done | bytes 9437200 | tf_op jit(solution)/shard_map/all_gather | solution.py:380
  590.8 152.8 %all-gather.46.cloned.1.call-done = bf16[1,8,768,768]{3,2,1,0:T(8,128)(2,1)} async-done(((bf16[1,8,192,768]{3,2,1,0:T(8,128)(2,1)}), bf16[1,8,768,768]{3,2,1,0:T(8,128)(2,1)}) %all-gather.46.cloned.1.call-update) | async-done | bytes 9437200 | tf_op jit(solution)/shard_map/all_gather | solution.py:379
  764.9 35.8 reduce-scatter.27.cloned.1.call-done
  816.2 20.2 all-gather.26.cloned.1.call-done
  845.0 229.7 %while.100 = (s32[]{:T(128)}, bf16[2,512,3,64]{1,3,2,0:T(8,128)(2,1)}, f32[2,3,512]{2,1,0:T(4,128)S(1)}, s32[2]{0:T(128)S(1)}, s32[1024]{0:T(1024)S(1)}, /*index...) while((s32[]{:T(128)}, ...), condition=%wide.region_19.20_spmd, body=%wide.region_16.19_spmd.sunk | while | flops 417430016 | bytes 143874384 | solution.py:79
  900.4 48.5 %rev.70 = f32[3,512,1024]{2,1,0:T(8,128)} reverse(f32[3,512,1024]{2,1,0:T(8,128)} %slice.252), dimensions={1} | reverse | bytes 12582912 | tf_op jit(solution)/shard_map/while/body/eval_jaxpr/rev | solution.py:37
  1015.0 48.5 %rev.70 = f32[3,512,1024]{2,1,0:T(8,128)} reverse(f32[3,512,1024]{2,1,0:T(8,128)} %slice.252), dimensions={1} | reverse | bytes 12582912 | tf_op jit(solution)/shard_map/while/body/eval_jaxpr/rev | solution.py:37
  1079.9 38.1 reduce-scatter.29.cloned.1.call-done
  1171.2 37.0 reduce-scatter.31.cloned.1.call-done
  1209.4 20.9 all-gather.34.cloned.1.call-done
  1265.5 38.0 reduce-scatter.37.cloned.1.call-done
  1330.6 515.9 %while.102 = (s32[]{:T(128)}, f32[1024,3,64]{0,2,1:T(8,128)}, f32[1024,3,64]{0,2,1:T(8,128)}, f32[3,2047]{1,0:T(4,128)S(1)}, bf16[2,512,3,64]{1,3,2,0:T(8,128)(2...) while((s32[]{:T(128)}, f32[1024,3,64]{0,2,1:T(8,128)}, ...), condition=%wide.region_54.55_spmd.clone, body=%wide.region_51.54_spmd.clone.sunk | while | flops 1027896320 | bytes 385841888 | solution.py:130
  1414.1 48.6 %rev.72 = f32[3,512,1024]{2,1,0:T(8,128)} reverse(f32[3,512,1024]{2,1,0:T(8,128)} %slice.254), dimensions={1} | reverse | bytes 12582912 | tf_op jit(solution)/shard_map/while/body/eval_jaxpr/rev | solution.py:37
  1481.0 48.6 %rev.73 = f32[3,512,1024]{2,1,0:T(8,128)} reverse(f32[3,512,1024]{2,1,0:T(8,128)} %subtract_multiply_fusion.6), dimensions={1} | reverse | bytes 12582912 | tf_op jit(solution)/shard_map/while/body/eval_jaxpr/rev | solution.py:43
  1658.4 48.6 %rev.72 = f32[3,512,1024]{2,1,0:T(8,128)} reverse(f32[3,512,1024]{2,1,0:T(8,128)} %slice.254), dimensions={1} | reverse | bytes 12582912 | tf_op jit(solution)/shard_map/while/body/eval_jaxpr/rev | solution.py:37
  1725.3 48.6 %rev.73 = f32[3,512,1024]{2,1,0:T(8,128)} reverse(f32[3,512,1024]{2,1,0:T(8,128)} %subtract_multiply_fusion.6), dimensions={1} | reverse | bytes 12582912 | tf_op jit(solution)/shard_map/while/body/eval_jaxpr/rev | solution.py:43
  1869.9 23.3 reduce-scatter.39.cloned.1.call-done
  1928.5 231.4 %while.101 = (s32[]{:T(128)}, bf16[2,512,3,64]{1,3,2,0:T(8,128)(2,1)}, f32[2,3,512]{2,1,0:T(4,128)S(1)}, s32[2]{0:T(128)S(1)}, s32[1024]{0:T(1024)S(1)}, /*index...) while((s32[]{:T(128)}, ...), condition=%wide.region_34.35_spmd, body=%wide.region_31.34_spmd.sunk | while | flops 417430016 | bytes 143874448 | solution.py:79
  1984.5 48.5 %rev.71 = f32[3,512,1024]{2,1,0:T(8,128)} reverse(f32[3,512,1024]{2,1,0:T(8,128)} %slice.253), dimensions={1} | reverse | bytes 12582912 | tf_op jit(solution)/shard_map/while/body/eval_jaxpr/rev | solution.py:37
  2099.9 48.5 %rev.71 = f32[3,512,1024]{2,1,0:T(8,128)} reverse(f32[3,512,1024]{2,1,0:T(8,128)} %slice.253), dimensions={1} | reverse | bytes 12582912 | tf_op jit(solution)/shard_map/while/body/eval_jaxpr/rev | solution.py:37
  2165.7 38.0 reduce-scatter.33.cloned.1.call-done
  2273.6 24.9 reduce-scatter.35.cloned.1.call-done
  2300.5 20.9 all-gather.38.cloned.1.call-done
  2356.3 38.0 reduce-scatter.41.cloned.1.call-done
  2422.5 517.2 %while.103 = (s32[]{:T(128)}, f32[1024,3,64]{0,2,1:T(8,128)}, f32[1024,3,64]{0,2,1:T(8,128)}, f32[3,2047]{1,0:T(4,128)S(1)}, bf16[2,512,3,64]{1,3,2,0:T(8,128)(2...) while((s32[]{:T(128)}, f32[1024,3,64]{0,2,1:T(8,128)}, ...), condition=%wide.region_67.68_spmd.clone, body=%wide.region_64.67_spmd.clone.sunk | while | flops 1027896320 | bytes 385841888 | solution.py:130
  2506.1 48.6 %rev.74 = f32[3,512,1024]{2,1,0:T(8,128)} reverse(f32[3,512,1024]{2,1,0:T(8,128)} %slice.256), dimensions={1} | reverse | bytes 12582912 | tf_op jit(solution)/shard_map/while/body/eval_jaxpr/rev | solution.py:37
  2573.0 48.6 %rev.75 = f32[3,512,1024]{2,1,0:T(8,128)} reverse(f32[3,512,1024]{2,1,0:T(8,128)} %subtract_multiply_fusion.7), dimensions={1} | reverse | bytes 12582912 | tf_op jit(solution)/shard_map/while/body/eval_jaxpr/rev | solution.py:43
  2750.4 48.6 %rev.74 = f32[3,512,1024]{2,1,0:T(8,128)} reverse(f32[3,512,1024]{2,1,0:T(8,128)} %slice.256), dimensions={1} | reverse | bytes 12582912 | tf_op jit(solution)/shard_map/while/body/eval_jaxpr/rev | solution.py:37
  2817.2 48.6 %rev.75 = f32[3,512,1024]{2,1,0:T(8,128)} reverse(f32[3,512,1024]{2,1,0:T(8,128)} %subtract_multiply_fusion.7), dimensions={1} | reverse | bytes 12582912 | tf_op jit(solution)/shard_map/while/body/eval_jaxpr/rev | solution.py:43
  2948.3 38.0 reduce-scatter.43.cloned.1.call-done
  3061.1 37.9 reduce-scatter.45.cloned.1.call-done
  3128.7 520.4 %while.104 = (s32[]{:T(128)}, f32[1024,3,64]{0,2,1:T(8,128)}, f32[1024,3,64]{0,2,1:T(8,128)}, f32[3,2047]{1,0:T(4,128)S(1)}, bf16[2,512,3,64]{1,3,2,0:T(8,128)(2...) while((s32[]{:T(128)}, f32[1024,3,64]{0,2,1:T(8,128)}, ...), condition=%wide.region_80.81_spmd.clone, body=%wide.region_77.80_spmd.clone.sunk | while | flops 1027896320 | bytes 384170688 | solution.py:130
  3213.2 48.5 %rev.76 = f32[3,512,1024]{2,1,0:T(8,128)} reverse(f32[3,512,1024]{2,1,0:T(8,128)} %slice.258), dimensions={1} | reverse | bytes 12582912 | tf_op jit(solution)/shard_map/while/body/eval_jaxpr/rev | solution.py:37
  3280.0 48.6 %rev.77 = f32[3,512,1024]{2,1,0:T(8,128)} reverse(f32[3,512,1024]{2,1,0:T(8,128)} %subtract_multiply_fusion.8), dimensions={1} | reverse | bytes 12582912 | tf_op jit(solution)/shard_map/while/body/eval_jaxpr/rev | solution.py:43
  3458.0 48.5 %rev.76 = f32[3,512,1024]{2,1,0:T(8,128)} reverse(f32[3,512,1024]{2,1,0:T(8,128)} %slice.258), dimensions={1} | reverse | bytes 12582912 | tf_op jit(solution)/shard_map/while/body/eval_jaxpr/rev | solution.py:37
  3524.7 48.6 %rev.77 = f32[3,512,1024]{2,1,0:T(8,128)} reverse(f32[3,512,1024]{2,1,0:T(8,128)} %subtract_multiply_fusion.8), dimensions={1} | reverse | bytes 12582912 | tf_op jit(solution)/shard_map/while/body/eval_jaxpr/rev | solution.py:43
  3683.0 25.5 multiply_add_fusion
  3794.6 23.1 multiply_add_fusion.1
  3849.3 33.3 all-reduce.12
  3888.7 154.2 %reduce-scatter.57.cloned.1.call-done = f32[8,768,192]{1,0,2:T(8,128)} async-done(((f32[8,768,768]{1,0,2:T(8,128)}), f32[8,768,192]{1,0,2:T(8,128)}) %reduce-scatter.57.cloned.1.call-update) | async-done | bytes 4718608 | tf_op jit(solution)/shard_map/reduce_scatter | solution.py:449
  4049.0 21.2 reduce-scatter.49.cloned.1.call-done
  4070.2 25.5 reduce-scatter.51.cloned.1.call-done
  4095.7 25.5 reduce-scatter.53.cloned.1.call-done
  4121.2 315.9 %reduce-scatter.55.cloned.1.call-done = f32[8,192,768]{2,1,0:T(8,128)} async-done(((f32[8,768,768]{2,1,0:T(8,128)}), f32[8,192,768]{2,1,0:T(8,128)}) %reduce-scatter.55.cloned.1.call-update) | async-done | bytes 4718608 | tf_op jit(solution)/shard_map/reduce_scatter | solution.py:448
  (1264 shorter events, 2025.4 us)
Async XLA Ops:
  7.2 757.4 %copy-start = (bf16[1,768,8]{1,2,0:T(8,128)(2,1)S(1)}, bf16[1,768,8]{1,2,0:T(8,128)(2,1)}, u32[]{:S(2)}) copy-start(bf16[1,768,8]{1,2,0:T(8,128)(2,1)} %param.36) | copy-start | bytes 36868
  7.2 87.0 %all-gather.22.cloned.1.call-start = ((), (), s32[]{:S(2)}) async-start(), calls=%async_computation.19 | async-start | bytes 1966080 | tf_op jit(solution)/shard_map/all_gather | solution.py:151
  11.1 374.9 %reduce-scatter.25.cloned.1.call-start = ((), (), s32[]{:S(2)}) async-start(), calls=%async_computation.20 | async-start | bytes 3932160 | tf_op jit(solution)/shard_map/reduce_scatter | solution.py:164
  347.6 60.7 %all-gather.24.cloned.1.call-start = ((), (), s32[]{:S(2)}) async-start(), calls=%async_computation.21 | async-start | bytes 1966080 | tf_op jit(solution)/shard_map/all_gather | solution.py:172
  387.4 413.4 %copy-start.30 = (f32[256,768]{1,0:T(8,128)}, f32[256,768]{1,0:T(8,128)S(1)}, u32[]{:S(2)}) copy-start(f32[256,768]{1,0:T(8,128)S(1)} %get-tuple-element.1223) | copy-start | bytes 2359300
  388.4 188.8 %all-gather.48.cloned.1.call-start = ((), (), s32[]{:S(2)}) async-start(), calls=%async_computation.49 | async-start | bytes 11796480 | tf_op jit(solution)/shard_map/all_gather | solution.py:380
  392.8 350.8 %all-gather.46.cloned.1.call-start = ((), (), s32[]{:S(2)}) async-start(), calls=%async_computation.48 | async-start | bytes 11796480 | tf_op jit(solution)/shard_map/all_gather | solution.py:379
  393.4 407.3 %reduce-scatter.27.cloned.1.call-start = ((), (), s32[]{:S(2)}) async-start(), calls=%async_computation.22 | async-start | bytes 3932160 | tf_op jit(solution)/shard_map/reduce_scatter | solution.py:193
  393.5 197.3 %copy-start.195 = (s32[1,1024,1]{1,2,0:T(1,128)}, s32[1,1024,1]{1,2,0:T(1,128)S(1)}, u32[]{:S(2)}) copy-start(s32[1,1024,1]{1,2,0:T(1,128)S(1)} %get-tuple-element.1261) | copy-start | bytes 12292
  401.9 188.9 %copy-start.230 = (s32[1024]{0:T(1024)}, s32[1024]{0:T(1024)S(1)}, u32[]{:S(2)}) copy-start(s32[1024]{0:T(1024)S(1)} %broadcast_select_fusion.32) | copy-start | bytes 12292
  764.5 71.9 %all-gather.26.cloned.1.call-start = ((), (), s32[]{:S(2)}) async-start(), calls=%async_computation.23 | async-start | bytes 1966080 | tf_op jit(solution)/shard_map/all_gather | solution.py:151
  802.1 11.7 collective-permute-start
  815.5 302.4 %reduce-scatter.29.cloned.1.call-start = ((), (), s32[]{:S(2)}) async-start(), calls=%async_computation.24 | async-start | bytes 3932160 | tf_op jit(solution)/shard_map/reduce_scatter | solution.py:164
  1074.7 233.3 %copy-start.193 = (f32[2,3,512]{2,1,0:T(4,128)}, f32[2,3,512]{2,1,0:T(4,128)S(1)}, u32[]{:S(2)}) copy-start(f32[2,3,512]{2,1,0:T(4,128)S(1)} %get-tuple-element.856) | copy-start | bytes 36868
  1079.8 61.2 %all-gather.28.cloned.1.call-start = ((), (), s32[]{:S(2)}) async-start(), calls=%async_computation.25 | async-start | bytes 1966080 | tf_op jit(solution)/shard_map/all_gather | solution.py:172
  1121.3 86.9 %reduce-scatter.31.cloned.1.call-start = ((), (), s32[]{:S(2)}) async-start(), calls=%async_computation.26 | async-start | bytes 3932160 | tf_op jit(solution)/shard_map/reduce_scatter | solution.py:193
  1170.0 60.3 %all-gather.34.cloned.1.call-start = ((), (), s32[]{:S(2)}) async-start(), calls=%async_computation.31 | async-start | bytes 1966080 | tf_op jit(solution)/shard_map/all_gather | solution.py:248
  1170.8 132.6 %copy-start.215 = (s32[256]{0:T(256)}, s32[256]{0:T(256)S(1)}, u32[]{:S(2)}) copy-start(s32[256]{0:T(256)S(1)} %dynamic_slice.219) | copy-start | bytes 3076
  1171.1 132.4 %copy-start.169 = (f32[256,8]{0,1:T(8,128)}, f32[256,8]{0,1:T(8,128)S(1)}, u32[]{:S(2)}) copy-start(f32[256,8]{0,1:T(8,128)S(1)} %get-tuple-element.1271) | copy-start | bytes 24580
  1171.1 132.4 %copy-start.200 = (f32[256]{0:T(256)}, f32[256]{0:T(256)S(1)}, u32[]{:S(2)}) copy-start(f32[256]{0:T(256)S(1)} %get-tuple-element.1270) | copy-start | bytes 3076
  1171.1 132.3 %copy-start.218 = (f32[256]{0:T(256)}, f32[256]{0:T(256)S(1)}, u32[]{:S(2)}) copy-start(f32[256]{0:T(256)S(1)} %fusion.346) | copy-start | bytes 3076
  1209.4 94.1 %reduce-scatter.37.cloned.1.call-start = ((), (), s32[]{:S(2)}) async-start(), calls=%async_computation.32 | async-start | bytes 3932160 | tf_op jit(solution)/shard_map/reduce_scatter | solution.py:266
  1265.4 62.4 %all-gather.36.cloned.1.call-start = ((), (), s32[]{:S(2)}) async-start(), calls=%async_computation.33 | async-start | bytes 1966080 | tf_op jit(solution)/shard_map/all_gather | solution.py:309
  1307.9 585.3 %reduce-scatter.39.cloned.1.call-start = ((), (), s32[]{:S(2)}) async-start(), calls=%async_computation.34 | async-start | bytes 3932160 | tf_op jit(solution)/shard_map/reduce_scatter | solution.py:334
  1855.1 64.7 %all-gather.30.cloned.1.call-start = ((), (), s32[]{:S(2)}) async-start(), calls=%async_computation.27 | async-start | bytes 1966080 | tf_op jit(solution)/shard_map/all_gather | solution.py:151
  1857.7 12.3 collective-permute-start.1
  1900.0 303.7 %reduce-scatter.33.cloned.1.call-start = ((), (), s32[]{:S(2)}) async-start(), calls=%async_computation.28 | async-start | bytes 3932160 | tf_op jit(solution)/shard_map/reduce_scatter | solution.py:164
  2165.7 62.1 %all-gather.32.cloned.1.call-start = ((), (), s32[]{:S(2)}) async-start(), calls=%async_computation.29 | async-start | bytes 1966080 | tf_op jit(solution)/shard_map/all_gather | solution.py:172
  2208.0 90.5 %reduce-scatter.35.cloned.1.call-start = ((), (), s32[]{:S(2)}) async-start(), calls=%async_computation.30 | async-start | bytes 3932160 | tf_op jit(solution)/shard_map/reduce_scatter | solution.py:193
  2260.4 60.9 %all-gather.38.cloned.1.call-start = ((), (), s32[]{:S(2)}) async-start(), calls=%async_computation.35 | async-start | bytes 1966080 | tf_op jit(solution)/shard_map/all_gather | solution.py:248
  2260.5 13.2 collective-permute-start.2
  2262.4 131.9 %copy-start.221 = (s32[1,256,1]{1,2,0:T(1,128)}, s32[1,256,1]{1,2,0:T(1,128)S(1)}, u32[]{:S(2)}) copy-start(s32[1,256,1]{1,2,0:T(1,128)S(1)} %constant_dynamic-slice_fusion.6) | copy-start | bytes 3076
  2262.7 131.7 %copy-start.167 = (f32[256,8]{0,1:T(8,128)}, f32[256,8]{0,1:T(8,128)S(1)}, u32[]{:S(2)}) copy-start(f32[256,8]{0,1:T(8,128)S(1)} %get-tuple-element.1274) | copy-start | bytes 24580
  2300.4 94.0 %reduce-scatter.41.cloned.1.call-start = ((), (), s32[]{:S(2)}) async-start(), calls=%async_computation.36 | async-start | bytes 3932160 | tf_op jit(solution)/shard_map/reduce_scatter | solution.py:266
  2356.3 63.3 %all-gather.40.cloned.1.call-start = ((), (), s32[]{:S(2)}) async-start(), calls=%async_computation.37 | async-start | bytes 1966080 | tf_op jit(solution)/shard_map/all_gather | solution.py:309
  2399.7 586.6 %reduce-scatter.43.cloned.1.call-start = ((), (), s32[]{:S(2)}) async-start(), calls=%async_computation.38 | async-start | bytes 3932160 | tf_op jit(solution)/shard_map/reduce_scatter | solution.py:334
  2948.2 77.5 %all-gather.42.cloned.1.call-start = ((), (), s32[]{:S(2)}) async-start(), calls=%async_computation.39 | async-start | bytes 1966080 | tf_op jit(solution)/shard_map/all_gather | solution.py:248
  2991.1 12.8 collective-permute-start.3
  3006.8 92.3 %reduce-scatter.45.cloned.1.call-start = ((), (), s32[]{:S(2)}) async-start(), calls=%async_computation.40 | async-start | bytes 3932160 | tf_op jit(solution)/shard_map/reduce_scatter | solution.py:266
  3060.9 61.7 %all-gather.44.cloned.1.call-start = ((), (), s32[]{:S(2)}) async-start(), calls=%async_computation.41 | async-start | bytes 1966080 | tf_op jit(solution)/shard_map/all_gather | solution.py:309
  3102.9 726.0 %reduce-scatter.61.cloned.1.call-start = ((), (), s32[]{:S(2)}) async-start(), calls=%async_computation.51 | async-start | bytes 417792
  3112.0 733.4 %reduce-scatter.59.cloned.1.call-start = ((), (), s32[]{:S(2)}) async-start(), calls=%async_computation.50 | async-start | bytes 983040
  3125.8 721.3 %reduce-scatter.47.cloned.1.call-start = ((), (), s32[]{:S(2)}) async-start(), calls=%async_computation.42 | async-start | bytes 3932160 | tf_op jit(solution)/shard_map/reduce_scatter | solution.py:334
  3658.1 384.9 %reduce-scatter.57.cloned.1.call-start = ((), (), s32[]{:S(2)}) async-start(), calls=%async_computation.47 | async-start | bytes 23592960 | tf_op jit(solution)/shard_map/reduce_scatter | solution.py:449
  3727.7 342.5 %reduce-scatter.49.cloned.1.call-start = ((), (), s32[]{:S(2)}) async-start(), calls=%async_computation.43 | async-start | bytes 983040 | tf_op jit(solution)/shard_map/reduce_scatter | solution.py:443
  3765.8 329.9 %reduce-scatter.51.cloned.1.call-start = ((), (), s32[]{:S(2)}) async-start(), calls=%async_computation.44 | async-start | bytes 983040 | tf_op jit(solution)/shard_map/reduce_scatter | solution.py:444
  3780.2 341.0 %reduce-scatter.53.cloned.1.call-start = ((), (), s32[]{:S(2)}) async-start(), calls=%async_computation.45 | async-start | bytes 983040 | tf_op jit(solution)/shard_map/reduce_scatter | solution.py:445
  3794.6 642.5 %reduce-scatter.55.cloned.1.call-start = ((), (), s32[]{:S(2)}) async-start(), calls=%async_computation.46 | async-start | bytes 23592960 | tf_op jit(solution)/shard_map/reduce_scatter | solution.py:448
  (332 other events, 8163.7 us)
Sparse Core Ops, SparseCore 0:
  11.2 22.3 all-gather.21
  347.7 38.2 reduce-scatter.24
  388.5 19.6 all-gather.23
  410.3 166.7 all-gather.47
  578.6 164.9 all-gather.45
  764.6 36.1 reduce-scatter.26
  815.6 20.6 all-gather.25
  1080.0 37.9 reduce-scatter.28
  1121.4 19.6 all-gather.27
  1170.1 37.9 reduce-scatter.30
  1210.3 20.0 all-gather.33
  1265.5 37.9 reduce-scatter.36
  1308.1 19.6 all-gather.35
  1855.2 37.9 reduce-scatter.38
  1900.2 19.6 all-gather.29
  2165.8 37.9 reduce-scatter.32
  2208.1 19.6 all-gather.31
  2260.5 37.9 reduce-scatter.34
  2300.5 20.7 all-gather.37
  2356.4 37.9 reduce-scatter.40
  2399.9 19.6 all-gather.39
  2948.3 37.9 reduce-scatter.42
  3006.9 18.7 all-gather.41
  3061.1 37.9 reduce-scatter.44
  3103.0 19.6 all-gather.43
  3126.4 55.5 reduce-scatter.60
  3184.2 22.3 reduce-scatter.58
  3658.2 37.9 reduce-scatter.46
  3727.8 315.1 reduce-scatter.56
  4045.7 24.4 reduce-scatter.48
  4073.1 22.5 reduce-scatter.50
  4098.6 22.5 reduce-scatter.52
  4124.0 313.0 reduce-scatter.54
where the time goes:
time: 4520 us; the launch traced here: 4440 us
  local copies, waits for them, and re-layouts  2100 us (46%)
  waiting for transfers between devices  1470 us (33%)
  matrix products  435 us (10%)
  other arithmetic  147 us (3%)
  loops' own time  139 us (3%)
  blocking collectives  123 us (3%)
    rev x12, local copies, waits for them, and re-layouts, skewed_bias(): return tiled[:, ::-1, :]  582 us
    while x290, local copies, waits for them, and re-layouts  501 us
    reduce_scatter x1, waiting for transfers between devices, per_device(): lax.psum_scatter(ffn_total[0], 'dp', scatter_dimension=1, tiled=True)  316 us
    rev x6, local copies, waits for them, and re-layouts, diagonal_sums(): flipped = grad_scores[:, ::-1, :]  292 us
    all_gather x1, waiting for transfers between devices, per_device(): lax.all_gather(sharded[6], 'dp', axis=2, tiled=True)  161 us
    reshape x12, local copies, waits for them, and re-layouts, skewed_bias(): jnp.broadcast_to(window[:, None, :], (head_count, block_len, span))  158 us
    reduce_scatter x1, waiting for transfers between devices, per_device(): lax.psum_scatter(ffn_total[1], 'dp', scatter_dimension=2, tiled=True)  154 us
    all_gather x1, waiting for transfers between devices, per_device(): lax.all_gather(sharded[5], 'dp', axis=1, tiled=True)  153 us
  transfers between devices with their start and end apart: 37, of which 33 were waited for; matrix products, arithmetic and copies ran while one was open for 17% of the time, Pallas kernels for 0%

commit v1 on v0

v1 whole, which is shorter than its diff:
```python
import functools

import jax
import jax.numpy as jnp
from jax import lax
from jax.experimental import pallas as pl
from jax.experimental.pallas import tpu as pltpu
from jax.sharding import PartitionSpec as P

BF = jnp.bfloat16
F32 = jnp.float32
BLOCK = 128
MASKED = -1e30


def shifted(value, axis, steps):
    count = lax.axis_size(axis)
    initial, last = (max(0, -steps), min(count, count - steps))
    return lax.ppermute(value, axis, [(source, source + steps) for source in range(initial, last)])


def normed(values, gain):
    return values * lax.rsqrt(jnp.mean(values * values, axis=-1, keepdims=True) + 1e-06) * gain


def traded(value, distance):
    count = lax.axis_size("mp")
    return lax.ppermute(value, "mp", [(place, place ^ distance) for place in range(count)])


def gather_rows(rows):
    if lax.axis_size("mp") != 4:
        return lax.all_gather(rows, "mp", axis=0, tiled=True)
    place = lax.axis_index("mp")
    low_y, low_core = place < 2, place % 2 == 0
    across = traded(rows, 2)
    own = jnp.stack([jnp.where(low_y, rows, across), jnp.where(low_y, across, rows)])
    other = traded(own, 1)
    both = jnp.stack([jnp.where(low_core, own, other), jnp.where(low_core, other, own)], axis=1)
    return both.reshape(4 * rows.shape[0], rows.shape[1])


def scatter_rows(parts):
    if lax.axis_size("mp") != 4:
        return lax.psum_scatter(parts.astype(F32), "mp", scatter_dimension=0, tiled=True)
    place = lax.axis_index("mp")
    low_y, low_core = place < 2, place % 2 == 0
    split = parts.reshape(2, 2, parts.shape[0] // 4, parts.shape[1])
    kept = jnp.where(low_core, split[:, 0], split[:, 1]).astype(F32)
    given = jnp.where(low_core, split[:, 1], split[:, 0]).astype(BF)
    pair = kept + traded(given, 1).astype(F32)
    mine = jnp.where(low_y, pair[0], pair[1])
    theirs = jnp.where(low_y, pair[1], pair[0]).astype(BF)
    return mine + traded(theirs, 2).astype(F32)


def skewed(bias_row, span):
    tiled = jnp.broadcast_to(bias_row, (BLOCK, span))
    return pltpu.roll(tiled, span - BLOCK + 1, 1, stride=1, stride_axis=0)


def folded(total):
    rows = total.shape[0]
    while rows > 8:
        rows //= 2
        total = pltpu.roll(total[:rows], rows, 1) + total[rows:]
    back = 7 - lax.broadcasted_iota(jnp.int32, total.shape, 0)
    for step in (4, 2, 1):
        total = jnp.where((back // step) % 2 == 1, pltpu.roll(total, step, 1), total)
    return jnp.sum(total, axis=0, keepdims=True)


def dot_t(left, right):
    return lax.dot_general(left, right, (((1,), (1,)), ((), ())), preferred_element_type=F32)


def dot_lead(left, right):
    return lax.dot_general(left, right, (((0,), (0,)), ((), ())), preferred_element_type=F32)


def attend_kernel(heads, qkv_ref, bias_ref, docs_row, docs_col, out_ref, lse_ref, skew, qs, ks, vs):
    group_len = qkv_ref.shape[0]
    width = qkv_ref.shape[1] // (3 * heads)
    scale = width ** (-0.5)
    span = bias_ref.shape[1]
    for h in range(heads):
        skew[h] = skewed(bias_ref[h : h + 1, :], span)
        qs[h] = (qkv_ref[:, h * width : (h + 1) * width].astype(F32) * scale).astype(BF)
        ks[h] = qkv_ref[:, (heads + h) * width : (heads + h + 1) * width]
        vs[h] = qkv_ref[:, (2 * heads + h) * width : (2 * heads + h + 1) * width]

    def block(number, carry):
        opening = pl.multiple_of(number * BLOCK, BLOCK)
        rows = pl.ds(opening, BLOCK)
        window = pl.ds(pl.multiple_of(group_len - BLOCK - opening, BLOCK), group_len)
        same = docs_col[rows, :] == docs_row[...]
        mixed, lse = [], []
        for h in range(heads):
            scores = dot_t(qs[h, rows, :], ks[h]) + skew[h, :, window]
            scores = jnp.where(same, scores, MASKED)
            top = jnp.max(scores, axis=-1, keepdims=True)
            expo = jnp.exp(scores - top)
            total = jnp.sum(expo, axis=-1, keepdims=True)
            probs = (expo * (1.0 / total)).astype(BF)
            mixed.append(jnp.dot(probs, vs[h], preferred_element_type=F32))
            lse.append(top + jnp.log(total))
        out_ref[rows, :] = jnp.concatenate(mixed, axis=1).astype(BF)
        lse_ref[rows, :] = jnp.concatenate(lse, axis=1)
        return carry

    lax.fori_loop(0, group_len // BLOCK, block, 0)


def attend_back_kernel(
    heads, qkv_ref, grad_ref, lse_ref, bias_ref, docs_row, docs_col,
    out_ref, grad_bias_ref, skew, total, qs, ks, vs, gs, dq, dk, dv,
):
    group_len = qkv_ref.shape[0]
    width = qkv_ref.shape[1] // (3 * heads)
    scale = width ** (-0.5)
    span = bias_ref.shape[1]
    for h in range(heads):
        skew[h] = skewed(bias_ref[h : h + 1, :], span)
        qs[h] = (qkv_ref[:, h * width : (h + 1) * width].astype(F32) * scale).astype(BF)
        ks[h] = qkv_ref[:, (heads + h) * width : (heads + h + 1) * width]
        vs[h] = qkv_ref[:, (2 * heads + h) * width : (2 * heads + h + 1) * width]
        gs[h] = grad_ref[:, h * width : (h + 1) * width]
    total[...] = jnp.zeros_like(total)
    dk[...] = jnp.zeros_like(dk)
    dv[...] = jnp.zeros_like(dv)

    def block(number, carry):
        opening = pl.multiple_of(number * BLOCK, BLOCK)
        rows = pl.ds(opening, BLOCK)
        window = pl.ds(pl.multiple_of(group_len - BLOCK - opening, BLOCK), group_len)
        same = docs_col[rows, :] == docs_row[...]
        lse = lse_ref[rows, :]
        for h in range(heads):
            query, grad = qs[h, rows, :], gs[h, rows, :]
            scores = dot_t(query, ks[h]) + skew[h, :, window]
            probs = jnp.exp(jnp.where(same, scores, MASKED) - lse[:, h : h + 1])
            grad_probs = dot_t(grad, vs[h])
            inner = jnp.sum(probs * grad_probs, axis=-1, keepdims=True)
            exact = probs * (grad_probs - inner)
            total[h, :, window] += exact
            rounded = exact.astype(BF)
            dq[h, rows, :] = jnp.dot(rounded, ks[h], preferred_element_type=F32) * scale
            dk[h] += dot_lead(rounded, query)
            dv[h] += dot_lead(probs.astype(BF), grad)
        return carry

    lax.fori_loop(0, group_len // BLOCK, block, 0)
    pieces = [part[h] for part in (dq, dk, dv) for h in range(heads)]
    out_ref[...] = jnp.concatenate(pieces, axis=1).astype(BF)
    for h in range(heads):
        grad_bias_ref[h : h + 1, :] = folded(total[h])


def attend(qkv, bias_off, documents):
    heads, span = bias_off.shape
    group_len, columns = qkv.shape
    width = columns // (3 * heads)
    rows = pltpu.VMEM((heads, group_len, width), BF)
    return pl.pallas_call(
        functools.partial(attend_kernel, heads),
        out_shape=(
            jax.ShapeDtypeStruct((group_len, heads * width), BF),
            jax.ShapeDtypeStruct((group_len, heads), F32),
        ),
        scratch_shapes=[pltpu.VMEM((heads, BLOCK, span), F32), rows, rows, rows],
        compiler_params=pltpu.CompilerParams(vmem_limit_bytes=40 * 2**20),
        cost_estimate=pl.CostEstimate(
            flops=heads * group_len * group_len * width * 16,
            bytes_accessed=qkv.size * 4,
            transcendentals=heads * group_len * group_len,
        ),
        name="attend",
    )(qkv, bias_off, documents[None, :], documents[:, None])


def attend_back(qkv, grad_mixed, lse, bias_off, documents):
    heads, span = bias_off.shape
    group_len, columns = qkv.shape
    width = columns // (3 * heads)
    skew = pltpu.VMEM((heads, BLOCK, span), F32)
    rows = pltpu.VMEM((heads, group_len, width), BF)
    wide = pltpu.VMEM((heads, group_len, width), F32)
    return pl.pallas_call(
        functools.partial(attend_back_kernel, heads),
        out_shape=(
            jax.ShapeDtypeStruct((group_len, columns), BF),
            jax.ShapeDtypeStruct((heads, span), F32),
        ),
        scratch_shapes=[skew, skew, rows, rows, rows, rows, wide, wide, wide],
        compiler_params=pltpu.CompilerParams(vmem_limit_bytes=48 * 2**20),
        cost_estimate=pl.CostEstimate(
            flops=heads * group_len * group_len * width * 40,
            bytes_accessed=qkv.size * 8,
            transcendentals=heads * group_len * group_len,
        ),
        name="attend_back",
    )(qkv, grad_mixed, lse, bias_off, documents[None, :], documents[:, None])


def layer_forward(layer_in, documents, chosen, weights, small, bias_off):
    w_qkv, w_out_t, w_in, w_out = weights
    gain_attn, gain_ffn, w_router = small
    row_count, width = layer_in.shape
    group_len = documents.shape[0]
    experts = w_in.shape[0]
    capacity = group_len // 4
    gathered = gather_rows(normed(layer_in, gain_attn).astype(BF))
    qkv = jnp.dot(gathered, w_qkv, preferred_element_type=F32).astype(BF)
    mixed, lse = attend(qkv, bias_off, documents)
    attn = scatter_rows(jnp.einsum("tc,dc->td", mixed, w_out_t, preferred_element_type=F32))
    hidden = layer_in + attn
    routed_loc = normed(hidden, gain_ffn).astype(BF)
    routed = gather_rows(routed_loc)
    router_prob = jax.nn.softmax(
        jnp.dot(routed_loc, w_router, preferred_element_type=F32), axis=-1
    )
    chosen_loc = lax.dynamic_slice_in_dim(
        chosen, lax.axis_index("mp") * row_count, row_count, 0
    )
    labels = jnp.arange(experts, dtype=jnp.int32)
    picked = (chosen_loc[:, None] == labels[None, :]).astype(F32)
    gate_prob = jnp.sum(router_prob * picked, axis=1, keepdims=True)
    named = (chosen[None, :] == labels[:, None]).astype(jnp.int32)
    rank = jnp.sum((jnp.cumsum(named, axis=1) - 1) * named, axis=0)
    slots = chosen * capacity + rank
    places = jnp.arange(experts * capacity, dtype=jnp.int32)
    dispatch = (slots[None, :] == places[:, None]).astype(BF)
    buffer = jnp.dot(dispatch, routed, preferred_element_type=F32).astype(BF)
    buffer = buffer.reshape(experts, capacity, width)
    inner = jnp.einsum("ecd,edf->ecf", buffer, w_in, preferred_element_type=F32)
    active = jax.nn.gelu(inner).astype(BF)
    partial = jnp.einsum("ecf,edf->ecd", active, w_out, preferred_element_type=F32).astype(BF)
    returned = lax.dot_general(
        dispatch,
        partial.reshape(experts * capacity, width),
        (((0,), (0,)), ((), ())),
        preferred_element_type=F32,
    )
    expert_out = scatter_rows(returned.astype(BF))
    result = hidden + gate_prob * expert_out
    kept = dict(
        layer_in=layer_in, gathered=gathered, qkv=qkv, lse=lse, mixed=mixed, hidden=hidden,
        routed_loc=routed_loc, router_prob=router_prob, picked=picked, gate_prob=gate_prob,
        expert_out=expert_out, inner=inner.astype(BF), active=active, buffer=buffer,
        slots=slots, documents=documents,
    )
    return (result, kept)


def layer_backward(grad_out, kept, weights, small, bias_off):
    w_qkv, w_out_t, w_in, w_out = weights
    gain_attn, gain_ffn, w_router = small
    experts, width, _ = w_in.shape
    capacity = kept["documents"].shape[0] // 4
    slots, gate_prob, router_prob = kept["slots"], kept["gate_prob"], kept["router_prob"]
    places = jnp.arange(experts * capacity, dtype=jnp.int32)
    dispatch = (slots[None, :] == places[:, None]).astype(BF)
    grad_expert = gather_rows((gate_prob * grad_out).astype(BF))
    grad_buffer = jnp.dot(dispatch, grad_expert, preferred_element_type=F32).astype(BF)
    grad_buffer = grad_buffer.reshape(experts, capacity, width)
    grad_active = jnp.einsum("ecd,edf->ecf", grad_buffer, w_out, preferred_element_type=F32)
    grad_inner = jax.vjp(jax.nn.gelu, kept["inner"].astype(F32))[1](grad_active)[0].astype(BF)
    grad_part = jnp.einsum(
        "ecf,edf->ecd", grad_inner, w_in, preferred_element_type=F32
    ).astype(BF)
    grad_part = lax.dot_general(
        dispatch,
        grad_part.reshape(experts * capacity, width),
        (((0,), (0,)), ((), ())),
        preferred_element_type=F32,
    )
    grad_routed = scatter_rows(grad_part.astype(BF))
    grad_gate = jnp.sum(grad_out * kept["expert_out"], axis=1, keepdims=True)
    grad_prob = kept["picked"] * grad_gate
    grad_logit = router_prob * (
        grad_prob - jnp.sum(router_prob * grad_prob, axis=1, keepdims=True)
    )
    grad_routed = grad_routed + jnp.dot(
        grad_logit, w_router.astype(F32).T, precision=lax.Precision.HIGHEST
    )
    grad_router = jnp.dot(
        kept["routed_loc"].astype(F32).T, grad_logit, precision=lax.Precision.HIGHEST
    )
    norm_back = jax.vjp(normed, kept["hidden"], gain_ffn)[1]
    grad_hidden_norm, grad_gain_ffn = norm_back(grad_routed)
    grad_hidden = grad_out + grad_hidden_norm

    grad_attn = gather_rows(grad_hidden.astype(BF))
    grad_mixed = jnp.dot(grad_attn, w_out_t, preferred_element_type=F32).astype(BF)
    grad_qkv, grad_bias = attend_back(
        kept["qkv"], grad_mixed, kept["lse"], bias_off, kept["documents"]
    )
    grad_normed = scatter_rows(
        jnp.einsum("tc,dc->td", grad_qkv, w_qkv, preferred_element_type=F32)
    )
    norm_back_attn = jax.vjp(normed, kept["layer_in"], gain_attn)[1]
    grad_in_norm, grad_gain_attn = norm_back_attn(grad_normed)
    grad_in = grad_hidden + grad_in_norm
    small_grads = jnp.concatenate(
        [grad_gain_attn[:, None], grad_gain_ffn[:, None], grad_router], axis=1
    )
    factors = dict(
        grad_buffer=grad_buffer, grad_inner=grad_inner, grad_attn=grad_attn,
        grad_qkv=grad_qkv, grad_bias=grad_bias, small=small_grads, grad_in=grad_in,
    )
    return factors


def per_device(
    inputs,
    cotangent,
    w_query,
    w_key,
    w_value,
    w_attn_out,
    rel_table,
    gain_attn,
    gain_ffn,
    w_router,
    w_expert_in,
    w_expert_out,
    doc_ids,
    expert_ids,
    buckets,
):
    micro = inputs.shape[0]
    is_first = lax.axis_index("section") == 0
    shards = lax.axis_size("dp")
    depth, columns = w_query.shape[1:]
    heads, bins = rel_table.shape[1:]
    width = depth * shards
    bundle = jnp.concatenate(
        [
            w_query[0],
            w_key[0],
            w_value[0],
            w_attn_out[0].T,
            jnp.pad(rel_table[0], ((0, 8 - heads), (0, columns - bins))),
        ],
        axis=0,
    )
    bundle = lax.all_gather(bundle, "dp", axis=0)
    w_in = lax.all_gather(w_expert_in[0], "dp", axis=1, tiled=True)
    w_out = lax.all_gather(jnp.swapaxes(w_expert_out[0], 1, 2), "dp", axis=1, tiled=True)
    square = [
        bundle[:, part * depth : (part + 1) * depth].reshape(width, columns) for part in range(4)
    ]
    w_qkv = jnp.concatenate(square[:3], axis=1)
    table = jnp.swapaxes(bundle[:, 4 * depth : 4 * depth + heads, :bins], 0, 1)
    table = table.reshape(heads, shards * bins)
    weights = (w_qkv, square[3], w_in, w_out)
    small = (gain_attn[0].astype(F32), gain_ffn[0].astype(F32), w_router[0])
    bucket_row = jnp.pad(buckets, (0, 1), constant_values=-1)
    onehot = (
        bucket_row[:, None] == jnp.arange(shards * bins, dtype=jnp.int32)[None, :]
    ).astype(F32)
    bias_off = jnp.dot(table.astype(F32), onehot.T, precision=lax.Precision.HIGHEST)

    def either(first, second):
        return jax.tree.map(lambda one, two: jnp.where(is_first, one, two), first, second)

    received = jnp.zeros(inputs.shape[1:], BF)
    results, stored = ([], [])
    for tick in range(micro + 1):
        early = min(tick, micro - 1)
        later = max(tick - 1, 0)
        layer_in = jnp.where(is_first, inputs[early], received).astype(F32)
        documents = jnp.where(is_first, doc_ids[early], doc_ids[later])
        chosen = jnp.where(is_first, expert_ids[early, :, 0], expert_ids[later, :, 0])
        result, kept = layer_forward(layer_in, documents, chosen, weights, small, bias_off)
        results.append(result)
        stored.append(kept)
        if tick < micro:
            received = shifted(result.astype(BF), "section", 1)
    returned = jnp.zeros(inputs.shape[1:], BF)
    factors = []
    for tick in range(micro + 1):
        kept = either(stored[max(tick - 1, 0)], stored[min(tick + 1, micro)])
        grad_out = jnp.where(is_first, returned, cotangent[min(tick, micro - 1)]).astype(F32)
        factors.append(layer_backward(grad_out, kept, weights, small, bias_off))
        if tick < micro:
            returned = shifted(factors[-1]["grad_in"].astype(BF), "section", -1)

    def forward_joined(name, axis):
        chosen_parts = [
            either(stored[index][name], stored[index + 1][name]) for index in range(micro)
        ]
        return jnp.concatenate(chosen_parts, axis=axis)

    def backward_parts(name):
        return [
            either(factors[index + 1][name], factors[index][name]) for index in range(micro)
        ]

    def backward_joined(name, axis):
        return jnp.concatenate(backward_parts(name), axis=axis)

    grad_w_out = jnp.einsum(
        "ecd,ecf->edf",
        backward_joined("grad_buffer", 1),
        forward_joined("active", 1),
        preferred_element_type=F32,
    ).astype(BF)
    grad_w_out = lax.psum_scatter(grad_w_out, "dp", scatter_dimension=1, tiled=True)
    grad_w_in = jnp.einsum(
        "ecd,ecf->edf",
        forward_joined("buffer", 1),
        backward_joined("grad_inner", 1),
        preferred_element_type=F32,
    ).astype(BF)
    grad_w_in = lax.psum_scatter(grad_w_in, "dp", scatter_dimension=1, tiled=True)
    grad_w_qkv = jnp.einsum(
        "td,tc->dc",
        forward_joined("gathered", 0),
        backward_joined("grad_qkv", 0),
        preferred_element_type=F32,
    )
    grad_w_out_t = jnp.einsum(
        "td,tc->dc",
        backward_joined("grad_attn", 0),
        forward_joined("mixed", 0),
        preferred_element_type=F32,
    )
    grad_table = jnp.dot(
        sum(backward_parts("grad_bias")), onehot, precision=lax.Precision.HIGHEST
    )
    grad_table = jnp.swapaxes(grad_table.reshape(heads, shards, bins), 0, 1)
    grad_bundle = jnp.concatenate(
        [grad_w_qkv[:, part * columns : (part + 1) * columns].reshape(shards, depth, columns)
         for part in range(3)]
        + [
            grad_w_out_t.reshape(shards, depth, columns),
            jnp.pad(grad_table, ((0, 0), (0, 8 - heads), (0, columns - bins))),
        ],
        axis=1,
    ).astype(BF)
    grad_bundle = lax.psum_scatter(grad_bundle, "dp", scatter_dimension=0).astype(F32)
    small_sum = lax.psum_scatter(
        sum(backward_parts("small")), ("dp", "mp"), scatter_dimension=0, tiled=True
    )
    outputs = jnp.stack(
        [jnp.where(is_first, results[index], results[index + 1]) for index in range(micro)]
    )
    grad_inputs = jnp.stack(backward_parts("grad_in"))
    return (
        outputs.astype(BF)[None],
        grad_inputs[None],
        grad_bundle[None, :depth],
        grad_bundle[None, depth : 2 * depth],
        grad_bundle[None, 2 * depth : 3 * depth],
        grad_bundle[3 * depth : 4 * depth].T[None],
        grad_bundle[None, 4 * depth : 4 * depth + heads, :bins],
        small_sum[None, :, 0],
        small_sum[None, :, 1],
        small_sum[None, :, 2:],
        grad_w_in.astype(F32)[None],
        jnp.swapaxes(grad_w_out, 1, 2).astype(F32)[None],
    )


def solution(mesh):
    placed = (
        P(None, ("dp", "mp"), None),
        P(None, ("dp", "mp"), None),
        P("section", "dp", "mp"),
        P("section", "dp", "mp"),
        P("section", "dp", "mp"),
        P("section", "mp", "dp"),
        P("section", "mp", "dp"),
        P("section", None),
        P("section", None),
        P("section", None, None),
        P("section", None, "dp", "mp"),
        P("section", None, "mp", "dp"),
        P(None, "dp"),
        P(None, "dp", None),
        P(),
    )
    return jax.shard_map(
        per_device,
        mesh=mesh,
        in_specs=placed,
        out_specs=(
            P("section", None, ("dp", "mp"), None),
            P("section", None, ("dp", "mp"), None),
            P("section", "dp", "mp"),
            P("section", "dp", "mp"),
            P("section", "dp", "mp"),
            P("section", "mp", "dp"),
            P("section", "mp", "dp"),
            P("section", ("dp", "mp")),
            P("section", ("dp", "mp")),
            P("section", ("dp", "mp"), None),
            P("section", None, "dp", "mp"),
            P("section", None, "mp", "dp"),
        ),
        check_vma=False,
    )
```

time: 4520 us -> 1450 us (0.32); the launches traced: 4440 us -> 1440 us
  local copies, waits for them, and re-layouts: 2100 us -> 70.3 us
  waiting for transfers between devices: 1470 us -> 899 us
  matrix products: 435 us -> 224 us
  loops' own time: 139 us -> 0 us
  blocking collectives: 123 us -> 0 us
  Pallas kernels: 0 us -> 103 us
  other arithmetic: 147 us -> 76.9 us
    rev x18 -> x0, local copies, waits for them, and re-layouts: 874 us -> none  [the longest x12 582 us: skewed_bias(): return tiled[:, ::-1, :]]
    reduce_scatter x17 -> x3, waiting for transfers between devices: 930 us -> 347 us  [the longest x1 160 us: per_device(): lax.psum_scatter(grad_w_in, 'dp', scatter_dimension=1, tiled=True)]
    while x293 -> x0, local copies, waits for them, and re-layouts: 506 us -> none
    reshape x18 -> x14, local copies, waits for them, and re-layouts: 251 us -> 12.4 us  [the longest x5 6.97 us: per_device(): bundle[:, part * depth:(part + 1) * depth].reshape(width, columns)]
    ppermute x0 -> x48, waiting for transfers between devices: none -> 234 us  [traded(): lax.ppermute(value, 'mp', [(place, place ^ distance) for place in range(c...]
    all_gather x14 -> x3, waiting for transfers between devices: 501 us -> 270 us  [the longest x1 156 us: per_device(): lax.all_gather(jnp.swapaxes(w_expert_out[0], 1, 2), 'dp', axis=1, tiled=T...]
    dot_general x109 -> x51, matrix products: 435 us -> 224 us  [the longest x3 47.7 us: layer_backward(): jnp.einsum('ecd,edf->ecf', grad_buffer, w_out, preferred_element_type=F32)]
    another operation x6 -> x0, loops' own time: 139 us -> none  [the longest x3 107 us: attend_back(): lax.scan(one_block, (zeros_rows, zeros_rows, start_bias), (openings, lse_...]
  transfers between devices with their start and end apart: 37 -> 59, of which waited for: 33 -> 56; matrix products, arithmetic and copies ran while one was open for 17% -> 9% of each run, Pallas kernels for 0% -> 1%
where the time goes in v1:
time: 1450 us; the launch traced here: 1440 us
  waiting for transfers between devices  899 us (62%)
  matrix products  224 us (15%)
  Pallas kernels  103 us (7%)
  other arithmetic  76.9 us (5%)
  local copies, waits for them, and re-layouts  70.3 us (5%)
  starting transfers between devices  51.9 us (4%)
  between operations  17.5 us (1%)
    ppermute x48, waiting for transfers between devices, traded(): lax.ppermute(value, 'mp', [(place, place ^ distance) for place in range(c...  234 us
    reduce_scatter x1, waiting for transfers between devices, per_device(): lax.psum_scatter(grad_w_in, 'dp', scatter_dimension=1, tiled=True)  160 us
    reduce_scatter x1, waiting for transfers between devices, per_device(): lax.psum_scatter(grad_w_out, 'dp', scatter_dimension=1, tiled=True)  156 us
    all_gather x1, waiting for transfers between devices, per_device(): lax.all_gather(jnp.swapaxes(w_expert_out[0], 1, 2), 'dp', axis=1, tiled=T...  156 us
    all_gather x1, waiting for transfers between devices, per_device(): w_in = lax.all_gather(w_expert_in[0], 'dp', axis=1, tiled=True)  94 us
    pallas_call x3, Pallas kernels, attend_back(): pl.pallas_call(functools.partial(attend_back_kernel, heads), out_shape=(j...  60.8 us
    dot_general x3, matrix products, layer_backward(): jnp.einsum('ecd,edf->ecf', grad_buffer, w_out, preferred_element_type=F32)  47.7 us
    pallas_call x3, Pallas kernels, attend(): pl.pallas_call(functools.partial(attend_kernel, heads), out_shape=(jax.Sh...  42.4 us
  transfers between devices with their start and end apart: 59, of which 56 were waited for; matrix products, arithmetic and copies ran while one was open for 9% of the time, Pallas kernels for 1%

profile of v1, /device:TPU:0, one launch (start us, length us, event | category | flops | bytes accessed | tf_op | source)
XLA Modules:
  0.0 1442.2 jit_solution(13358389757946200404)
XLA Ops:
  17.9 9.1 collective-permute-done
  30.1 19.5 %all-gather.11.cloned.1.call-done = bf16[4,776,192]{1,2,0:T(8,128)(2,1)} async-done(((bf16[1,776,192]{1,2,0:T(8,128)(2,1)}), bf16[4,776,192]{1,2,0:T(8,128)(2,1)}) %all-gather.11.cloned.1.call-update) | async-done | bytes 1191952 | tf_op jit(solution)/shard_map/all_gather | solution.py:347
  68.6 14.3 attend.3
  91.4 7.4 collective-permute-done.3
  122.9 94.0 %all-gather.9.cloned.1.call-done = bf16[1,8,768,768]{3,2,1,0:T(8,128)(2,1)} async-done(((bf16[1,8,192,768]{3,2,1,0:T(8,128)(2,1)}), bf16[1,8,768,768]{3,2,1,0:T(8,128)(2,1)}) %all-gather.9.cloned.1.call-update) | async-done | bytes 9437200 | tf_op jit(solution)/shard_map/all_gather | solution.py:348
  216.9 10.3 fusion.10
  227.2 156.3 %all-gather.7.cloned.1.call-done = bf16[8,768,768]{2,1,0:T(8,128)(2,1)} async-done(((bf16[8,192,768]{2,1,0:T(8,128)(2,1)}), bf16[8,768,768]{2,1,0:T(8,128)(2,1)}) %all-gather.7.cloned.1.call-update) | async-done | bytes 9437200 | tf_op jit(solution)/shard_map/all_gather | solution.py:349
  383.5 10.0 convolution_convert_fusion.4
  407.9 9.4 collective-permute-done.7
  421.9 7.6 collective-permute-done.8
  432.0 7.9 collective-permute-done.9
  449.9 13.8 attend.4
  468.7 9.7 collective-permute-done.12
  481.4 8.9 collective-permute-done.13
  503.9 10.0 convolution_convert_fusion.3
  524.3 9.4 collective-permute-done.16
  536.5 8.9 collective-permute-done.26
  553.8 10.6 fusion.35
  564.4 7.3 fusion.116
  579.9 9.7 collective-permute-done.29
  593.4 8.9 collective-permute-done.30
  613.5 20.3 %attend_back.3 = (bf16[1024,576]{1,0:T(8,128)(2,1)S(1)}, f32[3,2048]{1,0:T(4,128)S(1)}) custom-call(bf16[1024,576]{1,0:T(8,128)(2,1)S(1)} %copy-done.20, bf16[1024,192]{1,0:T(8,128)(2,1)S(1)} %copy.258.grad_ref, f32[1024,3]{1,0:T(8,128)S(1)} %broadcast_select_fusion.24.lse_ref, f32[3,2048]{1,0:T(4,128)S(1)} %fusion.144.bias_ref, ...), custom_call_target="tpu_custom_call" | custom-call | flops 8053063680 | bytes 4718592 | tf_op jit(solution)/shard_map/attend_back/pallas_call | solution.py:188
  656.1 8.6 collective-permute-done.18
  672.8 14.2 attend.5
  692.0 9.7 collective-permute-done.21
  706.9 8.9 collective-permute-done.22
  729.4 9.9 convolution_convert_fusion.2
  750.5 8.4 collective-permute-done.34
  762.7 8.9 collective-permute-done.35
  780.4 19.7 %broadcast_select_fusion.5 = (bf16[8,256,768]{2,1,0:T(8,128)(2,1)}, bf16[8,256,768]{2,1,0:T(8,128)(2,1)}, bf16[8,256,768]{2,1,0:T(8,128)(2,1)}) fusion(bf16[8,256,768]{2,1,0:T(8,128)(2,1)} %fusion.35, pred[]{:T(512)S(6)} %eq.235, f32[8,256,768]{2,1,0:T(8,128)} %fusion.6, f32[8,256,768]{2,1,0:T(8,128)} %fusion.10, f32[8,256,768]{2,1,0:T(8,128)} %fusion.8, ...), kind=kOutput, calls=%fused_computation.142 | convolution fusion | flops 2485125120 | bytes 44040192 | tf_op jit(solution)/shard_map/ecd,edf->ecf/dot_general | solution.py:266
  800.0 7.3 fusion.119
  815.5 9.7 collective-permute-done.38
  828.5 8.9 collective-permute-done.39
  844.7 20.2 %attend_back.4 = (bf16[1024,576]{1,0:T(8,128)(2,1)S(1)}, f32[3,2048]{1,0:T(4,128)S(1)}) custom-call(bf16[1024,576]{1,0:T(8,128)(2,1)S(1)} %copy-done.19, bf16[1024,192]{1,0:T(8,128)(2,1)S(1)} %copy.267.grad_ref, f32[1024,3]{1,0:T(8,128)S(1)} %copy-done.12, f32[3,2048]{1,0:T(4,128)S(1)} %fusion.144.bias_ref, s32[1,1024]{1,0:T(1,128)S(1)} %get-tuple-element.236.docs_row, ...), custom_call_target="tpu_custom_call" | custom-call | flops 8053063680 | bytes 4718592 | tf_op jit(solution)/shard_map/attend_back/pallas_call | solution.py:188
  870.7 9.7 collective-permute-done.42
  883.8 11.6 collective-permute-done.43
  897.3 8.3 collective-permute-done.44
  914.1 17.4 %broadcast_select_fusion.4 = (bf16[8,256,768]{2,1,0:T(8,128)(2,1)}, bf16[8,256,768]{2,1,0:T(8,128)(2,1)}, bf16[8,256,768]{2,1,0:T(8,128)(2,1)}) fusion(bf16[8,256,768]{2,1,0:T(8,128)(2,1)} %get-tuple-element.106, pred[]{:T(512)S(6)} %eq.235, f32[8,256,768]{2,1,0:T(8,128)} %fusion.6, f32[8,256,768]{2,1,0:T(8,128)S(1)} %bitcast.649, ...), kind=kOutput, calls=%fused_computation.141 | convolution fusion | flops 2485125120 | bytes 37748736 | tf_op jit(solution)/shard_map/ecd,edf->ecf/dot_general | solution.py:266
  947.3 9.7 collective-permute-done.47
  960.5 7.9 collective-permute-done.48
  977.8 20.2 %attend_back.5 = (bf16[1024,576]{1,0:T(8,128)(2,1)S(1)}, f32[3,2048]{1,0:T(4,128)S(1)}) custom-call(bf16[1024,576]{1,0:T(8,128)(2,1)S(1)} %copy-done.16, bf16[1024,192]{1,0:T(8,128)(2,1)S(1)} %copy.275.grad_ref, f32[1024,3]{1,0:T(8,128)S(1)} %copy-done.10, f32[3,2048]{1,0:T(4,128)S(1)} %fusion.144.bias_ref, s32[1,1024]{1,0:T(1,128)S(1)} %get-tuple-element.231.docs_row, ...), custom_call_target="tpu_custom_call" | custom-call | flops 8053063680 | bytes 4718592 | tf_op jit(solution)/shard_map/attend_back/pallas_call | solution.py:188
  1008.6 7.4 collective-permute-done.51
  1029.5 9.4 convolution_convert_fusion
  1042.3 9.4 convolution_convert_fusion.1
  1058.4 12.1 reduce-scatter.13.cloned.1.call-done
  1074.0 30.0 %reduce-scatter.7.cloned.1.call-done = bf16[1,776,192]{1,2,0:T(8,128)(2,1)} async-done(((bf16[4,776,192]{1,2,0:T(8,128)(2,1)}), bf16[1,776,192]{1,2,0:T(8,128)(2,1)}) %reduce-scatter.7.cloned.1.call-update) | async-done | bytes 298000 | tf_op jit(solution)/shard_map/reduce_scatter | solution.py:442
  1110.0 156.4 %reduce-scatter.11.cloned.1.call-done = bf16[8,192,768]{2,1,0:T(8,128)(2,1)} async-done(((bf16[8,768,768]{2,1,0:T(8,128)(2,1)}), bf16[8,192,768]{2,1,0:T(8,128)(2,1)}) %reduce-scatter.11.cloned.1.call-update) | async-done | bytes 2359312 | tf_op jit(solution)/shard_map/reduce_scatter | solution.py:409
  1270.7 160.2 %reduce-scatter.9.cloned.1.call-done = bf16[8,192,768]{2,1,0:T(8,128)(2,1)} async-done(((bf16[8,768,768]{2,1,0:T(8,128)(2,1)}), bf16[8,192,768]{2,1,0:T(8,128)(2,1)}) %reduce-scatter.9.cloned.1.call-update) | async-done | bytes 2359312 | tf_op jit(solution)/shard_map/reduce_scatter | solution.py:416
  (742 shorter events, 357.3 us)
Async XLA Ops:
  7.2 42.4 %all-gather.11.cloned.1.call-start = ((), (), s32[]{:S(2)}) async-start(), calls=%async_computation.9 | async-start | bytes 1720320 | tf_op jit(solution)/shard_map/all_gather | solution.py:347
  12.9 204.0 %all-gather.9.cloned.1.call-start = ((), (), s32[]{:S(2)}) async-start(), calls=%async_computation.8 | async-start | bytes 11796480 | tf_op jit(solution)/shard_map/all_gather | solution.py:348
  13.7 369.8 %all-gather.7.cloned.1.call-start = ((), (), s32[]{:S(2)}) async-start(), calls=%async_computation.4 | async-start | bytes 11796480 | tf_op jit(solution)/shard_map/all_gather | solution.py:349
  14.4 1056.0 %reduce-scatter.13.cloned.1.call-start = ((), (), s32[]{:S(2)}) async-start(), calls=%async_computation.10 | async-start | bytes 417792
  14.9 12.1 collective-permute-start
  27.4 2.4 collective-permute-start.1
  87.5 11.2 collective-permute-start.3
  100.7 10.6 collective-permute-start.4
  113.5 2.6 collective-permute-start.5
  401.4 2.6 collective-permute-start.6
  406.0 11.2 collective-permute-start.7
  418.3 11.2 collective-permute-start.8
  430.5 9.5 collective-permute-start.9
  441.3 2.6 collective-permute-start.10
  467.2 11.2 collective-permute-start.12
  479.9 10.4 collective-permute-start.13
  490.6 2.4 collective-permute-start.14
  522.5 11.2 collective-permute-start.16
  535.0 10.4 collective-permute-start.26
  545.6 2.4 collective-permute-start.27
  575.7 2.4 collective-permute-start.28
  578.4 11.2 collective-permute-start.29
  591.9 10.3 collective-permute-start.30
  603.3 2.6 collective-permute-start.31
  635.4 6.3 collective-permute-start.32
  637.1 13.2 collective-permute-start.17
  642.1 10.9 collective-permute-start.33
  654.6 10.1 collective-permute-start.18
  665.1 2.4 collective-permute-start.19
  690.5 11.2 collective-permute-start.21
  705.5 10.4 collective-permute-start.22
  716.0 2.4 collective-permute-start.23
  745.5 13.4 collective-permute-start.34
  748.0 11.2 collective-permute-start.25
  761.2 10.4 collective-permute-start.35
  814.0 11.2 collective-permute-start.38
  827.0 10.4 collective-permute-start.39
  869.2 11.2 collective-permute-start.42
  882.5 12.9 collective-permute-start.43
  895.8 9.8 collective-permute-start.44
  945.7 11.2 collective-permute-start.47
  958.1 10.4 collective-permute-start.48
  968.7 5.3 collective-permute-start.49
  1000.8 3.5 collective-permute-start.50
  1004.6 11.3 collective-permute-start.51
  1017.4 86.6 %reduce-scatter.7.cloned.1.call-start = ((), (), s32[]{:S(2)}) async-start(), calls=%async_computation.5 | async-start | bytes 1720320 | tf_op jit(solution)/shard_map/reduce_scatter | solution.py:442
  1025.8 240.6 %reduce-scatter.11.cloned.1.call-start = ((), (), s32[]{:S(2)}) async-start(), calls=%async_computation.7 | async-start | bytes 11796480 | tf_op jit(solution)/shard_map/reduce_scatter | solution.py:409
  1038.9 392.0 %reduce-scatter.9.cloned.1.call-start = ((), (), s32[]{:S(2)}) async-start(), calls=%async_computation.6 | async-start | bytes 11796480 | tf_op jit(solution)/shard_map/reduce_scatter | solution.py:416
  (187 other events, 3520.2 us)
Sparse Core Ops, SparseCore 0:
  13.1 36.5 all-gather.10
  51.2 165.7 all-gather.8
  218.5 164.9 all-gather.6
  1017.5 52.8 reduce-scatter.12
  1072.7 31.2 reduce-scatter.6
  1106.2 160.1 reduce-scatter.10
  1268.7 162.1 reduce-scatter.8

commit v2 on v1

--- a/solution.py
+++ b/solution.py
@@ -202,6 +202,30 @@
     )(qkv, grad_mixed, lse, bias_off, documents[None, :], documents[:, None])
 
 
+def undispatched(dispatch, slotted):
+    rows = slotted.reshape(dispatch.shape[0], slotted.shape[-1])
+    return lax.dot_general(
+        dispatch, rows, (((0,), (0,)), ((), ())), preferred_element_type=F32
+    ).astype(BF)
+
+
+def own_columns(rows):
+    shards = lax.axis_size("dp")
+    columns = rows.shape[1] // shards
+    every = lax.all_gather(rows, "dp", axis=0)
+    every = lax.dynamic_slice_in_dim(every, lax.axis_index("dp") * columns, columns, 2)
+    joined = gather_rows(every.reshape(-1, columns))
+    joined = joined.reshape(-1, shards, rows.shape[0], columns)
+    return jnp.swapaxes(joined, 0, 1).reshape(-1, columns)
+
+
+def expert_products(columns, named, rows):
+    spread = columns[:, None, :] * named[:, :, None]
+    spread = spread.reshape(columns.shape[0], -1)
+    product = dot_lead(spread, rows)
+    return product.reshape(named.shape[1], columns.shape[1], rows.shape[1])
+
+
 def layer_forward(layer_in, documents, chosen, weights, small, bias_off):
     w_qkv, w_out_t, w_in, w_out = weights
     gain_attn, gain_ffn, w_router = small
@@ -247,12 +271,12 @@
         layer_in=layer_in, gathered=gathered, qkv=qkv, lse=lse, mixed=mixed, hidden=hidden,
         routed_loc=routed_loc, router_prob=router_prob, picked=picked, gate_prob=gate_prob,
         expert_out=expert_out, inner=inner.astype(BF), active=active, buffer=buffer,
-        slots=slots, documents=documents,
+        active_rows=undispatched(dispatch, active), slots=slots, documents=documents,
     )
     return (result, kept)
 
 
-def layer_backward(grad_out, kept, weights, small, bias_off):
+def layer_backward(grad_out, kept, weights, small, bias_off, arrived=()):
     w_qkv, w_out_t, w_in, w_out = weights
     gain_attn, gain_ffn, w_router = small
     experts, width, _ = w_in.shape
@@ -260,7 +284,8 @@
     slots, gate_prob, router_prob = kept["slots"], kept["gate_prob"], kept["router_prob"]
     places = jnp.arange(experts * capacity, dtype=jnp.int32)
     dispatch = (slots[None, :] == places[:, None]).astype(BF)
-    grad_expert = gather_rows((gate_prob * grad_out).astype(BF))
+    grad_expert_loc = (gate_prob * grad_out).astype(BF)
+    grad_expert = gather_rows(grad_expert_loc)
     grad_buffer = jnp.dot(dispatch, grad_expert, preferred_element_type=F32).astype(BF)
     grad_buffer = grad_buffer.reshape(experts, capacity, width)
     grad_active = jnp.einsum("ecd,edf->ecf", grad_buffer, w_out, preferred_element_type=F32)
@@ -289,6 +314,7 @@
     norm_back = jax.vjp(normed, kept["hidden"], gain_ffn)[1]
     grad_hidden_norm, grad_gain_ffn = norm_back(grad_routed)
     grad_hidden = grad_out + grad_hidden_norm
+    grad_hidden, arrived = lax.optimization_barrier((grad_hidden, arrived))
 
     grad_attn = gather_rows(grad_hidden.astype(BF))
     grad_mixed = jnp.dot(grad_attn, w_out_t, preferred_element_type=F32).astype(BF)
@@ -307,6 +333,7 @@
     factors = dict(
         grad_buffer=grad_buffer, grad_inner=grad_inner, grad_attn=grad_attn,
         grad_qkv=grad_qkv, grad_bias=grad_bias, small=small_grads, grad_in=grad_in,
+        arrived=arrived, grad_expert_loc=grad_expert_loc, grad_inner_rows=undispatched(dispatch, grad_inner),
     )
     return factors
 
@@ -379,10 +406,29 @@
             received = shifted(result.astype(BF), "section", 1)
     returned = jnp.zeros(inputs.shape[1:], BF)
     factors = []
+    by_tokens = shards <= 4
+    forward_sides, backward_sides = [], []
+
+    def tokens_of(values, first, second, columns_name, rows_name):
+        columns = own_columns(either(values[first][columns_name], values[second][columns_name]))
+        rows = either(values[first][rows_name], values[second][rows_name])
+        return columns, lax.all_gather(rows, "dp", axis=0, tiled=True)
+
     for tick in range(micro + 1):
         kept = either(stored[max(tick - 1, 0)], stored[min(tick + 1, micro)])
         grad_out = jnp.where(is_first, returned, cotangent[min(tick, micro - 1)]).astype(F32)
-        factors.append(layer_backward(grad_out, kept, weights, small, bias_off))
+        arrived = ()
+        if by_tokens and tick >= 1:
+            side = tokens_of(stored, tick - 1, tick, "routed_loc", "active_rows")
+            grad_out, side = lax.optimization_barrier((grad_out, side))
+            forward_sides.append(side)
+        if by_tokens and tick >= 2:
+            arrived = tokens_of(
+                factors, tick - 1, tick - 2, "grad_expert_loc", "grad_inner_rows"
+            )
+        factors.append(layer_backward(grad_out, kept, weights, small, bias_off, arrived))
+        if by_tokens and tick >= 2:
+            backward_sides.append(factors[-1]["arrived"])
         if tick < micro:
             returned = shifted(factors[-1]["grad_in"].astype(BF), "section", -1)
 
@@ -400,20 +446,24 @@
     def backward_joined(name, axis):
         return jnp.concatenate(backward_parts(name), axis=axis)
 
-    grad_w_out = jnp.einsum(
-        "ecd,ecf->edf",
-        backward_joined("grad_buffer", 1),
-        forward_joined("active", 1),
-        preferred_element_type=F32,
-    ).astype(BF)
-    grad_w_out = lax.psum_scatter(grad_w_out, "dp", scatter_dimension=1, tiled=True)
-    grad_w_in = jnp.einsum(
-        "ecd,ecf->edf",
-        forward_joined("buffer", 1),
-        backward_joined("grad_inner", 1),
-        preferred_element_type=F32,
-    ).astype(BF)
-    grad_w_in = lax.psum_scatter(grad_w_in, "dp", scatter_dimension=1, tiled=True)
+    late = ()
+    if by_tokens:
+        late = tokens_of(factors, micro, micro - 1, "grad_expert_loc", "grad_inner_rows")
+    else:
+        grad_w_out = jnp.einsum(
+            "ecd,ecf->edf",
+            backward_joined("grad_buffer", 1),
+            forward_joined("active", 1),
+            preferred_element_type=F32,
+        ).astype(BF)
+        grad_w_out = lax.psum_scatter(grad_w_out, "dp", scatter_dimension=1, tiled=True)
+        grad_w_in = jnp.einsum(
+            "ecd,ecf->edf",
+            forward_joined("buffer", 1),
+            backward_joined("grad_inner", 1),
+            preferred_element_type=F32,
+        ).astype(BF)
+        grad_w_in = lax.psum_scatter(grad_w_in, "dp", scatter_dimension=1, tiled=True)
     grad_w_qkv = jnp.einsum(
         "td,tc->dc",
         forward_joined("gathered", 0),
@@ -439,9 +489,23 @@
         ],
         axis=1,
     ).astype(BF)
+    small_parts = sum(backward_parts("small"))
+    grad_bundle, small_parts, late = lax.optimization_barrier((grad_bundle, small_parts, late))
+    if by_tokens:
+        experts = w_in.shape[0]
+        labels = jnp.arange(experts, dtype=jnp.int32)
+        chosen_all = lax.all_gather(expert_ids[:, :, 0].astype(BF), "dp", axis=1, tiled=True)
+        named = (chosen_all.astype(jnp.int32)[:, :, None] == labels).astype(BF)
+        backward_sides.append(late)
+        grad_w_in, grad_w_out = 0.0, 0.0
+        for index in range(micro):
+            routed_cols, active_rows = forward_sides[index]
+            expert_cols, inner_rows = backward_sides[index]
+            grad_w_out += expert_products(expert_cols, named[index], active_rows)
+            grad_w_in += expert_products(routed_cols, named[index], inner_rows)
     grad_bundle = lax.psum_scatter(grad_bundle, "dp", scatter_dimension=0).astype(F32)
     small_sum = lax.psum_scatter(
-        sum(backward_parts("small")), ("dp", "mp"), scatter_dimension=0, tiled=True
+        small_parts, ("dp", "mp"), scatter_dimension=0, tiled=True
     )
     outputs = jnp.stack(
         [jnp.where(is_first, results[index], results[index + 1]) for index in range(micro)]

time: 1450 us -> 1360 us (0.938)
  waiting for transfers between devices: 899 us -> 636 us
  local copies, waits for them, and re-layouts: 70.3 us -> 138 us
  matrix products: 224 us -> 267 us
  other arithmetic: 76.9 us -> 118 us
    reduce_scatter x2 -> x0, waiting for transfers between devices: 317 us -> none  [the longest x1 160 us: per_device(): lax.psum_scatter(grad_w_in, 'dp', scatter_dimension=1, tiled=True)]
    all_gather x0 -> x8, waiting for transfers between devices: none -> 116 us  [the longest x4 85.1 us: tokens_of(): return (columns, lax.all_gather(rows, 'dp', axis=0, tiled=True))]
    dot_general x2 -> x10, matrix products: 18.8 us -> 84 us  [the longest x4 54.3 us: dot_lead(): lax.dot_general(left, right, (((0,), (0,)), ((), ())), preferred_element_...]
    ppermute x48 -> x56, waiting for transfers between devices: 234 us -> 197 us  [traded(): lax.ppermute(value, 'mp', [(place, place ^ distance) for place in range(c...]
    dot_general x3, matrix products: 47.7 us -> 20.4 us  [layer_backward(): jnp.einsum('ecd,edf->ecf', grad_buffer, w_out, preferred_element_type=F32)]
    reshape x0 -> x8, local copies, waits for them, and re-layouts: none -> 21.4 us  [the longest x4 15.6 us: own_columns(): return jnp.swapaxes(joined, 0, 1).reshape(-1, columns)]
    transpose x0 -> x4, local copies, waits for them, and re-layouts: none -> 18.4 us  [own_columns(): return jnp.swapaxes(joined, 0, 1).reshape(-1, columns)]
    another operation x2 -> x6, local copies, waits for them, and re-layouts: 0.57 us -> 16 us  [the longest x4 15.4 us: own_columns(): joined = joined.reshape(-1, shards, rows.shape[0], columns)]
  transfers between devices with their start and end apart: 59 -> 73, of which waited for: 56 -> 50; matrix products, arithmetic and copies ran while one was open for 9% -> 29% of each run, Pallas kernels for 1% -> 5%
where the time goes in v2:
time: 1360 us; the launch traced here: 1350 us
  waiting for transfers between devices  636 us (47%)
  matrix products  267 us (20%)
  local copies, waits for them, and re-layouts  138 us (10%)
  other arithmetic  118 us (9%)
  Pallas kernels  102 us (8%)
  starting transfers between devices  57.7 us (4%)
  between operations  17.9 us (1%)
    ppermute x56, waiting for transfers between devices, traded(): lax.ppermute(value, 'mp', [(place, place ^ distance) for place in range(c...  197 us
    all_gather x1, waiting for transfers between devices, per_device(): lax.all_gather(jnp.swapaxes(w_expert_out[0], 1, 2), 'dp', axis=1, tiled=T...  156 us
    all_gather x1, waiting for transfers between devices, per_device(): w_in = lax.all_gather(w_expert_in[0], 'dp', axis=1, tiled=True)  98.1 us
    all_gather x4, waiting for transfers between devices, tokens_of(): return (columns, lax.all_gather(rows, 'dp', axis=0, tiled=True))  85.1 us
    pallas_call x3, Pallas kernels, attend_back(): pl.pallas_call(functools.partial(attend_back_kernel, heads), out_shape=(j...  60.5 us
    dot_general x4, matrix products, dot_lead(): lax.dot_general(left, right, (((0,), (0,)), ((), ())), preferred_element_...  54.3 us
    ppermute x56, starting transfers between devices, traded(): lax.ppermute(value, 'mp', [(place, place ^ distance) for place in range(c...  45.9 us
    pallas_call x3, Pallas kernels, attend(): pl.pallas_call(functools.partial(attend_kernel, heads), out_shape=(jax.Sh...  41.7 us
  transfers between devices with their start and end apart: 73, of which 50 were waited for; matrix products, arithmetic and copies ran while one was open for 29% of the time, Pallas kernels for 5%

profile of v2, /device:TPU:0, one launch (start us, length us, event | category | flops | bytes accessed | tf_op | source)
XLA Modules:
  0.0 1350.0 jit_solution(14275051152297558328)
XLA Ops:
  17.9 9.1 collective-permute-done
  32.6 17.1 %all-gather.40.cloned.1.call-done = bf16[4,776,192]{1,2,0:T(8,128)(2,1)} async-done(((bf16[1,776,192]{1,2,0:T(8,128)(2,1)}), bf16[4,776,192]{1,2,0:T(8,128)(2,1)}) %all-gather.40.cloned.1.call-update) | async-done | bytes 1191952 | tf_op jit(solution)/shard_map/all_gather | solution.py:374
  63.4 14.1 %attend.3 = (bf16[1024,192]{1,0:T(8,128)(2,1)S(1)}, f32[1024,3]{1,0:T(8,128)S(1)}) custom-call(bf16[1024,576]{1,0:T(8,128)(2,1)S(1)} %convolution_convert_fusion.5.qkv_ref, f32[3,2048]{1,0:T(4,128)S(1)} %fusion.182.bias_ref, s32[1,1024]{1,0:T(1,128)S(1)} %get-tuple-element.286.docs_row, s32[1024,1]{1,0:T(8,128)S(1)} %copy.324.docs_col), custom_call_target="tpu_custom_call" | custom-call | flops 3221225472 | bytes 2359296 | tf_op jit(solution)/shard_map/attend/pallas_call | solution.py:164
  85.9 7.5 collective-permute-done.3
  118.8 98.1 %all-gather.30.cloned.1.call-done = bf16[1,8,768,768]{3,2,1,0:T(8,128)(2,1)} async-done(((bf16[1,8,192,768]{3,2,1,0:T(8,128)(2,1)}), bf16[1,8,768,768]{3,2,1,0:T(8,128)(2,1)}) %all-gather.30.cloned.1.call-update) | async-done | bytes 9437200 | tf_op jit(solution)/shard_map/all_gather | solution.py:375
  216.9 10.7 fusion.61
  227.7 155.8 %all-gather.20.cloned.1.call-done = bf16[8,768,768]{2,1,0:T(8,128)(2,1)} async-done(((bf16[8,192,768]{2,1,0:T(8,128)(2,1)}), bf16[8,768,768]{2,1,0:T(8,128)(2,1)}) %all-gather.20.cloned.1.call-update) | async-done | bytes 9437200 | tf_op jit(solution)/shard_map/all_gather | solution.py:376
  383.5 7.3 convolution_convert_fusion.2
  403.3 9.3 collective-permute-done.7
  417.3 7.6 collective-permute-done.8
  427.5 7.9 collective-permute-done.9
  445.4 13.8 %attend.4 = (bf16[1024,192]{1,0:T(8,128)(2,1)S(1)}, f32[1024,3]{1,0:T(8,128)S(1)}) custom-call(bf16[1024,576]{1,0:T(8,128)(2,1)S(1)} %get-tuple-element.307.qkv_ref, f32[3,2048]{1,0:T(4,128)S(1)} %fusion.182.bias_ref, s32[1,1024]{1,0:T(1,128)S(1)} %get-tuple-element.289.docs_row, s32[1024,1]{1,0:T(8,128)S(1)} %get-tuple-element.232.docs_col), custom_call_target="tpu_custom_call" | custom-call | flops 3221225472 | bytes 2359296 | tf_op jit(solution)/shard_map/attend/pallas_call | solution.py:164
  464.2 9.7 collective-permute-done.12
  476.8 8.9 collective-permute-done.13
  497.3 11.4 convolution_convert_fusion.1
  517.3 9.4 collective-permute-done.16
  529.5 8.9 collective-permute-done.26
  545.9 7.6 fusion.53
  553.5 11.6 fusion.140
  573.4 9.7 collective-permute-done.29
  586.4 8.9 collective-permute-done.30
  606.5 20.1 %attend_back.3 = (bf16[1024,576]{1,0:T(8,128)(2,1)S(1)}, f32[3,2048]{1,0:T(4,128)S(1)}) custom-call(bf16[1024,576]{1,0:T(8,128)(2,1)S(1)} %copy-done.21, bf16[1024,192]{1,0:T(8,128)(2,1)S(1)} %copy.358.grad_ref, f32[1024,3]{1,0:T(8,128)S(1)} %broadcast_select_fusion.24.lse_ref, f32[3,2048]{1,0:T(4,128)S(1)} %fusion.182.bias_ref, ...), custom_call_target="tpu_custom_call" | custom-call | flops 8053063680 | bytes 4718592 | tf_op jit(solution)/shard_map/attend_back/pallas_call | solution.py:188
  675.5 13.8 %attend.5 = (bf16[1024,192]{1,0:T(8,128)(2,1)S(1)}, f32[1024,3]{1,0:T(8,128)S(1)}) custom-call(bf16[1024,576]{1,0:T(8,128)(2,1)S(1)} %get-tuple-element.308.qkv_ref, f32[3,2048]{1,0:T(4,128)S(1)} %fusion.182.bias_ref, s32[1,1024]{1,0:T(1,128)S(1)} %get-tuple-element.285.docs_row, s32[1024,1]{1,0:T(8,128)S(1)} %copy.336.docs_col), custom_call_target="tpu_custom_call" | custom-call | flops 3221225472 | bytes 2359296 | tf_op jit(solution)/shard_map/attend/pallas_call | solution.py:164
  694.4 9.9 collective-permute-done.21
  712.5 7.8 collective-permute-done.22
  738.7 11.6 convolution_convert_fusion
  778.6 7.4 collective-permute-done.34
  794.7 9.0 collective-permute-done.37
  805.7 6.3 broadcast_select_fusion.6
  812.1 13.3 all-gather.6
  831.6 6.4 fusion.50
  838.1 10.1 fusion.143
  889.0 20.0 %attend_back.4 = (bf16[1024,576]{1,0:T(8,128)(2,1)S(1)}, f32[3,2048]{1,0:T(4,128)S(1)}) custom-call(bf16[1024,576]{1,0:T(8,128)(2,1)S(1)} %copy-done.18, bf16[1024,192]{1,0:T(8,128)(2,1)S(1)} %copy.370.grad_ref, f32[1024,3]{1,0:T(8,128)S(1)} %copy-done.13, f32[3,2048]{1,0:T(4,128)S(1)} %fusion.182.bias_ref, s32[1,1024]{1,0:T(1,128)S(1)} %get-tuple-element.288.docs_row, ...), custom_call_target="tpu_custom_call" | custom-call | flops 8053063680 | bytes 4718592 | tf_op jit(solution)/shard_map/attend_back/pallas_call | solution.py:188
  923.4 7.5 collective-permute-done.46
  932.2 6.3 collective-permute-done.44
  963.9 14.1 %all-gather.24.cloned.1.call-done = bf16[4096,768]{1,0:T(8,128)(2,1)} async-done(((bf16[1024,768]{1,0:T(8,128)(2,1)}), bf16[4096,768]{1,0:T(8,128)(2,1)}) %all-gather.24.cloned.1.call-update) | async-done | bytes 6291472 | tf_op jit(solution)/shard_map/all_gather | solution.py:415
  982.9 8.2 collective-permute-done.48
  1001.7 6.4 fusion.47
  1008.1 10.1 fusion.146
  1054.2 39.0 %all-gather.26.cloned.1.call-done = bf16[4096,768]{1,0:T(8,128)(2,1)} async-done(((bf16[1024,768]{1,0:T(8,128)(2,1)}), bf16[4096,768]{1,0:T(8,128)(2,1)}) %all-gather.26.cloned.1.call-update) | async-done | bytes 6291472 | tf_op jit(solution)/shard_map/all_gather | solution.py:415
  1099.0 30.9 %all-gather.38.cloned.1.call-done = bf16[1024,768]{1,0:T(8,128)(2,1)} async-done(((bf16[256,768]{1,0:T(8,128)(2,1)}), bf16[1024,768]{1,0:T(8,128)(2,1)}) %all-gather.38.cloned.1.call-update) | async-done | bytes 1572880 | tf_op jit(solution)/shard_map/all_gather | solution.py:215
  1151.7 20.4 %attend_back.5 = (bf16[1024,576]{1,0:T(8,128)(2,1)S(1)}, f32[3,2048]{1,0:T(4,128)S(1)}) custom-call(bf16[1024,576]{1,0:T(8,128)(2,1)S(1)} %copy-done.14, bf16[1024,192]{1,0:T(8,128)(2,1)S(1)} %copy.384.grad_ref, f32[1024,3]{1,0:T(8,128)S(1)} %copy-done.11, f32[3,2048]{1,0:T(4,128)S(1)} %fusion.182.bias_ref, s32[1,1024]{1,0:T(1,128)S(1)} %get-tuple-element.282.docs_row, ...), custom_call_target="tpu_custom_call" | custom-call | flops 8053063680 | bytes 4718592 | tf_op jit(solution)/shard_map/attend_back/pallas_call | solution.py:188
  1215.3 31.1 %all-gather.28.cloned.1.call-done = bf16[4096,768]{1,0:T(8,128)(2,1)} async-done(((bf16[1024,768]{1,0:T(8,128)(2,1)}), bf16[4096,768]{1,0:T(8,128)(2,1)}) %all-gather.28.cloned.1.call-update) | async-done | bytes 6291472 | tf_op jit(solution)/shard_map/all_gather | solution.py:415
  1248.7 13.8 %fusion.4 = f32[8,192,768]{2,1,0:T(8,128)} fusion(bf16[4096,768]{1,0:T(8,128)(2,1)} %all-gather.28.cloned.1.call-done, bf16[4096,8]{0,1:T(8,128)(2,1)S(1)} %copy-done.151, bf16[4096,192]{0,1:T(8,128)(2,1)} %reshape.920), kind=kOutput, calls=%fused_computation.4 | convolution fusion | flops 9669967872 | bytes 12648448 | tf_op jit(solution)/shard_map/dot_general | solution.py:78
  1262.5 15.6 %fusion = f32[8,192,768]{2,1,0:T(8,128)S(1)} fusion(bf16[4096,768]{1,0:T(8,128)(2,1)} %all-gather.24.cloned.1.call-done, bf16[4096,192]{0,1:T(8,128)(2,1)S(1)} %copy-done.110, bf16[4096,8]{0,1:T(8,128)(2,1)S(1)} %copy-done.151), kind=kOutput, calls=%fused_computation | convolution fusion | flops 9669967872 | bytes 12648448 | tf_op jit(solution)/shard_map/dot_general | solution.py:78
  1278.1 13.3 add_bitcast_fusion.1
  1291.4 11.7 add_bitcast_fusion
  1307.1 30.2 %reduce-scatter.5.cloned.1.call-done = bf16[1,776,192]{1,2,0:T(8,128)(2,1)} async-done(((bf16[4,776,192]{1,2,0:T(8,128)(2,1)}), bf16[1,776,192]{1,2,0:T(8,128)(2,1)}) %reduce-scatter.5.cloned.1.call-update) | async-done | bytes 298000 | tf_op jit(solution)/shard_map/reduce_scatter | solution.py:506
  (940 shorter events, 493.9 us)
Async XLA Ops:
  7.2 42.4 %all-gather.40.cloned.1.call-start = ((), (), s32[]{:S(2)}) async-start(), calls=%async_computation.13 | async-start | bytes 1720320 | tf_op jit(solution)/shard_map/all_gather | solution.py:374
  12.9 204.0 %all-gather.30.cloned.1.call-start = ((), (), s32[]{:S(2)}) async-start(), calls=%async_computation.8 | async-start | bytes 11796480 | tf_op jit(solution)/shard_map/all_gather | solution.py:375
  13.7 369.8 %all-gather.20.cloned.1.call-start = ((), (), s32[]{:S(2)}) async-start(), calls=%async_computation.2 | async-start | bytes 11796480 | tf_op jit(solution)/shard_map/all_gather | solution.py:376
  14.4 695.2 %all-gather.32.cloned.1.call-start = ((), (), s32[]{:S(2)}) async-start(), calls=%async_computation.9 | async-start | bytes 1966080 | tf_op jit(solution)/shard_map/all_gather | solution.py:215
  14.9 12.1 collective-permute-start
  82.1 11.3 collective-permute-start.3
  95.4 10.5 collective-permute-start.4
  401.5 11.2 collective-permute-start.7
  413.7 11.2 collective-permute-start.8
  462.6 11.2 collective-permute-start.12
  515.5 11.2 collective-permute-start.16
  528.0 10.4 collective-permute-start.26
  571.9 11.2 collective-permute-start.29
  584.9 10.4 collective-permute-start.30
  630.2 12.3 collective-permute-start.17
  636.5 11.2 collective-permute-start.33
  638.0 149.3 %all-gather.22.cloned.1.call-start = ((), (), s32[]{:S(2)}) async-start(), calls=%async_computation.3 | async-start | bytes 7864320 | tf_op jit(solution)/shard_map/all_gather | solution.py:415
  668.4 248.1 %all-gather.34.cloned.1.call-start = ((), (), s32[]{:S(2)}) async-start(), calls=%async_computation.10 | async-start | bytes 1966080 | tf_op jit(solution)/shard_map/all_gather | solution.py:215
  692.9 11.5 collective-permute-start.21
  708.2 12.1 collective-permute-start.22
  711.9 15.3 %collective-permute-start.35 = (bf16[1024,192]{0,1:T(8,128)(2,1)}, bf16[1024,192]{0,1:T(8,128)(2,1)S(1)}, u32[]{:S(2)}, u32[]{:S(2)}) collective-permute-start(bf16[1024,192]{0,1:T(8,128)(2,1)} %copy.412), channel_id=1, source_target_pairs={{0,2},{1,3},{2,0},{3,1},{4,6},{5,7},{6,4},{7,5},{8,10},{9,11},{10,... | collective-permute-start | bytes 1179656 | tf_op jit(solution)/shard_map/ppermute | solution.py:28
  729.1 28.6 %collective-permute-start.36 = (bf16[2,1024,192]{1,2,0:T(8,128)(2,1)}, bf16[2,1024,192]{1,2,0:T(8,128)(2,1)}, u32[]{:S(2)}, u32[]{:S(2)}) collective-permute-start(bf16[2,1024,192]{1,2,0:T(8,128)(2,1)} %pad_maximum_fusion.25), channel_id=1, source_target_pairs={{0,1},{1,0},{2,3},{3,2},{4,5},{5,4},{6,7},{7,6},{8,9},{9,8},{10,11... | collective-permute-start | bytes 2359304 | tf_op jit(solution)/shard_map/ppermute | solution.py:28
  756.5 17.8 %collective-permute-start.24 = (bf16[2,256,768]{2,1,0:T(8,128)(2,1)}, bf16[2,256,768]{2,1,0:T(8,128)(2,1)}, u32[]{:S(2)}, u32[]{:S(2)}) collective-permute-start(bf16[2,256,768]{2,1,0:T(8,128)(2,1)} %select_bitcast_fusion.24), channel_id=1, source_target_pairs={{0,1},{1,0},{2,3},{3,2},{4,5},{5,4},{6,7},{7,6},{8,9},{9,8},{10,11... | collective-permute-start | bytes 2359304 | tf_op jit(solution)/shard_map/ppermute | solution.py:28
  757.7 198.5 %all-gather.36.cloned.1.call-start = ((), (), s32[]{:S(2)}) async-start(), calls=%async_computation.11 | async-start | bytes 1966080 | tf_op jit(solution)/shard_map/all_gather | solution.py:215
  772.9 13.1 collective-permute-start.34
  777.1 11.4 collective-permute-start.25
  793.1 184.9 %all-gather.24.cloned.1.call-start = ((), (), s32[]{:S(2)}) async-start(), calls=%async_computation.4 | async-start | bytes 7864320 | tf_op jit(solution)/shard_map/all_gather | solution.py:415
  793.2 10.5 collective-permute-start.37
  805.7 19.7 %collective-permute-start.38 = (bf16[2,256,768]{2,1,0:T(8,128)(2,1)}, bf16[2,256,768]{2,1,0:T(8,128)(2,1)}, u32[]{:S(2)}, u32[]{:S(2)}) collective-permute-start(bf16[2,256,768]{2,1,0:T(8,128)(2,1)} %pad_maximum_fusion.26), channel_id=1, source_target_pairs={{0,1},{1,0},{2,3},{3,2},{4,5},{5,4},{6,7},{7,6},{8,9},{9,8},{10,11... | collective-permute-start | bytes 2359304 | tf_op jit(solution)/shard_map/ppermute | solution.py:28
  812.0 281.2 %all-gather.26.cloned.1.call-start = ((), (), s32[]{:S(2)}) async-start(), calls=%async_computation.5 | async-start | bytes 7864320 | tf_op jit(solution)/shard_map/all_gather | solution.py:415
  854.9 11.2 collective-permute-start.40
  868.8 10.6 collective-permute-start.41
  875.6 254.3 %all-gather.38.cloned.1.call-start = ((), (), s32[]{:S(2)}) async-start(), calls=%async_computation.12 | async-start | bytes 1966080 | tf_op jit(solution)/shard_map/all_gather | solution.py:215
  918.8 12.2 collective-permute-start.46
  922.8 15.7 %collective-permute-start.44 = (bf16[256,768]{1,0:T(8,128)(2,1)S(1)}, bf16[256,768]{1,0:T(8,128)(2,1)S(1)}, u32[]{:S(2)}, u32[]{:S(2)}) collective-permute-start(bf16[256,768]{1,0:T(8,128)(2,1)S(1)} %fusion.227), channel_id=1, source_target_pairs={{0,2},{1,3},{2,0},{3,1},{4,6},{5,7},{6,4},{7,5},{8,10},{9,11},{10,... | collective-permute-start | bytes 1179656 | tf_op jit(solution)/shard_map/ppermute | solution.py:28
  941.0 20.8 %collective-permute-start.45 = (bf16[256,768]{1,0:T(8,128)(2,1)}, bf16[256,768]{1,0:T(8,128)(2,1)}, u32[]{:S(2)}, u32[]{:S(2)}) collective-permute-start(bf16[256,768]{1,0:T(8,128)(2,1)} %convert_element_type.602), channel_id=1, source_target_pairs={{16,0},{17,1},{18,2},{19,3},{20,4},{21,5},{22,6},{23,7},{24,8},{25... | collective-permute-start | bytes 1179656 | tf_op jit(solution)/shard_map/ppermute | solution.py:19
  960.3 21.2 %collective-permute-start.52 = (bf16[1024,192]{0,1:T(8,128)(2,1)}, bf16[1024,192]{0,1:T(8,128)(2,1)}, u32[]{:S(2)}, u32[]{:S(2)}) collective-permute-start(bf16[1024,192]{0,1:T(8,128)(2,1)} %copy.414), channel_id=1, source_target_pairs={{0,2},{1,3},{2,0},{3,1},{4,6},{5,7},{6,4},{7,5},{8,10},{9,11},{10,... | collective-permute-start | bytes 1179656 | tf_op jit(solution)/shard_map/ppermute | solution.py:28
  980.0 11.1 collective-permute-start.48
  982.8 11.2 collective-permute-start.53
  995.3 251.1 %all-gather.28.cloned.1.call-start = ((), (), s32[]{:S(2)}) async-start(), calls=%async_computation.6 | async-start | bytes 7864320 | tf_op jit(solution)/shard_map/all_gather | solution.py:415
  1029.9 273.6 %reduce-scatter.7.cloned.1.call-start = ((), (), s32[]{:S(2)}) async-start(), calls=%async_computation.14 | async-start | bytes 417792
  1032.2 18.4 %collective-permute-start.51 = (bf16[256,768]{1,0:T(8,128)(2,1)S(1)}, bf16[256,768]{1,0:T(8,128)(2,1)S(1)}, u32[]{:S(2)}, u32[]{:S(2)}) collective-permute-start(bf16[256,768]{1,0:T(8,128)(2,1)S(1)} %fusion.228), channel_id=1, source_target_pairs={{0,2},{1,3},{2,0},{3,1},{4,6},{5,7},{6,4},{7,5},{8,10},{9,11},{10,... | collective-permute-start | bytes 1179656 | tf_op jit(solution)/shard_map/ppermute | solution.py:28
  1095.1 40.5 %collective-permute-start.54 = (bf16[256,768]{1,0:T(8,128)(2,1)}, bf16[256,768]{1,0:T(8,128)(2,1)}, u32[]{:S(2)}, u32[]{:S(2)}) collective-permute-start(bf16[256,768]{1,0:T(8,128)(2,1)} %convert_element_type.619), channel_id=1, source_target_pairs={{0,2},{1,3},{2,0},{3,1},{4,6},{5,7},{6,4},{7,5},{8,10},{9,11},{10,... | collective-permute-start | bytes 1179656 | tf_op jit(solution)/shard_map/ppermute | solution.py:28
  1134.1 11.0 collective-permute-start.58
  1146.2 51.2 %collective-permute-start.59 = (bf16[2,1024,192]{1,2,0:T(8,128)(2,1)}, bf16[2,1024,192]{1,2,0:T(8,128)(2,1)}, u32[]{:S(2)}, u32[]{:S(2)}) collective-permute-start(bf16[2,1024,192]{1,2,0:T(8,128)(2,1)} %pad_maximum_fusion.32), channel_id=1, source_target_pairs={{0,1},{1,0},{2,3},{3,2},{4,5},{5,4},{6,7},{7,6},{8,9},{9,8},{10,11... | collective-permute-start | bytes 2359304 | tf_op jit(solution)/shard_map/ppermute | solution.py:28
  1176.2 16.4 %collective-permute-start.56 = (bf16[2,256,768]{2,1,0:T(8,128)(2,1)}, bf16[2,256,768]{2,1,0:T(8,128)(2,1)}, u32[]{:S(2)}, u32[]{:S(2)}) collective-permute-start(bf16[2,256,768]{2,1,0:T(8,128)(2,1)} %fusion.203), channel_id=1, source_target_pairs={{0,1},{1,0},{2,3},{3,2},{4,5},{5,4},{6,7},{7,6},{8,9},{9,8},{10,11... | collective-permute-start | bytes 2359304 | tf_op jit(solution)/shard_map/ppermute | solution.py:28
  1195.9 16.7 %collective-permute-start.57 = (bf16[256,768]{1,0:T(8,128)(2,1)}, bf16[256,768]{1,0:T(8,128)(2,1)}, u32[]{:S(2)}, u32[]{:S(2)}) collective-permute-start(bf16[256,768]{1,0:T(8,128)(2,1)} %fusion.229), channel_id=1, source_target_pairs={{0,2},{1,3},{2,0},{3,1},{4,6},{5,7},{6,4},{7,5},{8,10},{9,11},{10,... | collective-permute-start | bytes 1179656 | tf_op jit(solution)/shard_map/ppermute | solution.py:28
  1247.3 90.0 %reduce-scatter.5.cloned.1.call-start = ((), (), s32[]{:S(2)}) async-start(), calls=%async_computation.7 | async-start | bytes 1720320 | tf_op jit(solution)/shard_map/reduce_scatter | solution.py:506
  (255 other events, 6700.4 us)
Sparse Core Ops, SparseCore 0:
  13.1 36.5 all-gather.39
  51.2 165.7 all-gather.29
  218.5 164.9 all-gather.19
  638.1 33.4 all-gather.31
  673.0 114.2 all-gather.21
  788.7 35.7 all-gather.33
  826.1 35.9 all-gather.35
  863.7 114.1 all-gather.23
  979.5 113.5 all-gather.25
  1094.6 35.3 all-gather.37
  1132.1 114.2 all-gather.27
  1249.7 53.7 reduce-scatter.6
  1305.9 31.2 reduce-scatter.4
